TPU v7x, 256 devices: a whole 4x4x8 slice. The times are simulated.
256 devices in a mesh: seq: 32 (over x, z_lo, core), head: 8 (over y, z_hi).
Axes of the slice: x: 4, y: 4, z: 8 (z_hi: 2, z_lo: 4; z = z_hi * 4 + z_lo), core: 2. Of those that a mesh axis runs over, the one named last changes fastest.
Arguments:
- tokens: bfloat16 [20480, 6144], P('seq'), may hold values from -6 to 6
- w_qkv: bfloat16 [3, 6144, 4096], P(None, 'seq', 'head'), may hold values from -0.07782233 to 0.07782233
- log_decay: float32 [32, 20480], P('head', 'seq'), may hold values from -0.7 to 0, as said below
- gain: float32 [4096], P('head'), may hold values from 0.5 to 1.5
Outputs:
- normed: bfloat16 [20480, 4096], P('seq', 'head')
Inputs may be any that keep to these rules, and one draw needn't show every extreme that they name: `log_decay`: every entry is negative.
All inputs are finite; a program needn't handle non-finite values.
Results may differ from a plain program's by a relative error of at most 0.0061.
Values may be sent and summed in bfloat16 or wider, within the bound.
No kernel may reach another device: no remote copies, remote signals or barrier semaphores. Data moves between devices by JAX's collectives and lax.ppermute only.
A program may use at most 128 MiB of HBM per device.

v0:
```python
import functools

import jax
import jax.numpy as jnp
from jax import lax
from jax.experimental import pallas as pl
from jax.experimental.pallas import tpu as pltpu
from jax.sharding import Mesh, PartitionSpec as P

HEAD_COUNT = 32
DH = 128
TAIL = 16
F32, BF16 = jnp.float32, jnp.bfloat16
NEXT = [(i, (i + 1) % 4) for i in range(4)]
LAST = [(i, (i - 1) % 4) for i in range(4)]
SWAP = [(0, 1), (1, 0)]
VMEM_LIMIT = 48 * 1024 * 1024


def tied(value, *others):
    return lax.optimization_barrier((value, others))[0]


def gather_kv(own):
    half = own.shape[0] // 2
    slots, opposite = [], None
    for distance in range(4):
        if distance:
            own = lax.ppermute(own, "zl", NEXT)
        right, left = lax.ppermute(own, "x", NEXT), lax.ppermute(own, "x", LAST)
        if distance in (1, 2):
            opposite = lax.ppermute(opposite, "zl", NEXT)
        else:
            opposite = jnp.concatenate([lax.ppermute(right[:half], "x", NEXT), lax.ppermute(left[half:], "x", LAST)])
        slots.append((own, right, left, opposite))
    return slots


def gather_q(own):
    columns = [own]
    for _ in range(3):
        columns.append(lax.ppermute(columns[-1], "zl", NEXT))
    column = jnp.concatenate(columns)
    half = column.shape[0] // 2
    right, left = lax.ppermute(column, "x", NEXT), lax.ppermute(column, "x", LAST)
    return [column, right, left], [lax.ppermute(right[:half], "x", NEXT), lax.ppermute(left[half:], "x", LAST)]


def project_body(count, chunks, parts, has_acc, index_ref, *refs):
    mine, theirs, weights = refs[:chunks], refs[chunks : 2 * chunks], refs[2 * chunks : 2 * chunks + parts]
    out_ref = refs[-1]
    tile = mine[0].shape[0]
    rows = jnp.concatenate(
        [jnp.concatenate([ref[...] for ref in mine], axis=1), jnp.concatenate([ref[...] for ref in theirs], axis=1)], axis=0
    )
    for c in range(count):
        cuts = [ref.shape[0] // count for ref in weights]
        w = jnp.concatenate([ref[c * cut : (c + 1) * cut, :] for ref, cut in zip(weights, cuts)], axis=0)
        total = jnp.dot(rows, w, preferred_element_type=F32)
        for place in range(2):
            part = total[place * tile : (place + 1) * tile]
            if has_acc:
                part = part + refs[-2][place, c]
            out_ref[place, c] = part.astype(out_ref.dtype)


def project(count, depth, index, mine, theirs, weights, acc, last):
    rows, width = mine.shape[0], weights[0].shape[1]
    tile, chunks, parts = rows // 4, len(index), len(weights)
    token_specs = [pl.BlockSpec((tile, depth), functools.partial(lambda n, i, ref: (i, ref[n]), n)) for n in range(chunks)]
    weight_specs = [pl.BlockSpec(part.shape, lambda i, ref: (0, 0)) for part in weights]
    acc_spec = pl.BlockSpec((2, count, tile, width), lambda i, ref: (0, 0, i, 0))
    return pl.pallas_call(
        functools.partial(project_body, count, chunks, parts, acc is not None),
        out_shape=jax.ShapeDtypeStruct((2, count, rows, width), BF16 if last else F32),
        grid_spec=pltpu.PrefetchScalarGridSpec(
            num_scalar_prefetch=1,
            grid=(4,),
            in_specs=token_specs * 2 + weight_specs + ([] if acc is None else [acc_spec]),
            out_specs=acc_spec,
        ),
        compiler_params=pltpu.CompilerParams(vmem_limit_bytes=VMEM_LIMIT),
        cost_estimate=pl.CostEstimate(
            flops=4 * rows * depth * chunks * count * width, bytes_accessed=4 * rows * depth * chunks, transcendentals=0
        ),
    )(jnp.stack(index), *([mine] * chunks), *([theirs] * chunks), *weights, *([] if acc is None else [acc]))


def join(earlier, later):
    return jnp.exp(later[1])[:, None, :] * earlier[0] + later[0], earlier[1] + later[1]


def split(value, count):
    parts = []
    for _ in range(count):
        parts.append(value.astype(BF16).astype(F32))
        value = value - parts[-1]
    return parts


def unpack(ref, mask=None):
    state, total = ref[:, :DH, :].astype(F32), jnp.sum(ref[:, DH:, :].astype(F32), axis=1)
    if mask is not None:
        state, total = state * mask, total * mask
    return state, total


def pack(ref, value):
    ref[:, :DH, :] = value[0].astype(ref.dtype)
    row = lax.broadcasted_iota(jnp.int32, (ref.shape[0], TAIL, DH), 1)
    tail = jnp.zeros(row.shape, F32)
    for n, part in enumerate(split(value[1], 3)):
        tail = jnp.where(row == n, part[:, None, :], tail)
    ref[:, DH:, :] = tail.astype(ref.dtype)


def state_body(place_ref, kv_ref, column_ref, total_ref, chip_ref, sent_ref, first_ref):
    group = chip_ref.shape[0]
    second_mine = place_ref[0].astype(F32)
    states, totals = [], []
    for place in range(2):
        total = jnp.stack([total_ref[place, h, 0] for h in range(group)])
        local = []
        for h in range(group):
            cut = slice(h * DH, (h + 1) * DH)
            decay = jnp.exp(total[h : h + 1, :1] - column_ref[place, h])
            keys = (kv_ref[place, 0, :, cut].astype(F32) * decay).astype(BF16)
            local.append(
                lax.dot_general(keys, kv_ref[place, 1, :, cut], (((0,), (0,)), ((), ())), preferred_element_type=F32)
            )
        states.append(jnp.stack(local))
        totals.append(total)
    first = [jnp.where(second_mine > 0, v[1], v[0]) for v in (states, totals)]
    second = [jnp.where(second_mine > 0, v[0], v[1]) for v in (states, totals)]
    pack(first_ref, first)
    both = join(first, second)
    pack(chip_ref, both)
    pack(sent_ref, both)


def row_body(z_ref, own_ref, back1, back2, back3, before_ref, row_ref):
    z = z_ref[0]
    backs = [back1, back2, back3]
    before = [unpack(ref, (j + 1 <= z).astype(F32)) for j, ref in enumerate(backs)]
    after = [unpack(ref, (j + 1 > z).astype(F32)) for j, ref in enumerate(backs)]
    prefix = join(join(before[2], before[1]), before[0])
    suffix = join(join(after[2], after[1]), after[0])
    pack(before_ref, prefix)
    pack(row_ref, join(join(prefix, unpack(own_ref)), suffix))


def incoming_body(place_ref, before_ref, first_ref, back1, back2, back3, out_ref):
    rows = join(join(unpack(back3), unpack(back2)), unpack(back1))
    state = join(rows, unpack(before_ref))[0]
    first = unpack(first_ref)
    later = jnp.exp(first[1])[:, None, :] * state + first[0]
    mine_second = place_ref[0].astype(F32)
    for place, value in enumerate(
        (jnp.where(mine_second > 0, later, state), jnp.where(mine_second > 0, state, later))
    ):
        for n, part in enumerate(split(value, 3)):
            out_ref[place, :, n * DH : (n + 1) * DH, :] = part.astype(BF16)


def small_kernel(body, outs, scalar, *args):
    return pl.pallas_call(
        body,
        out_shape=[jax.ShapeDtypeStruct(*out) for out in outs],
        in_specs=[pl.BlockSpec(memory_space=pltpu.SMEM)] + [pl.BlockSpec(memory_space=pltpu.VMEM)] * len(args),
        out_specs=[pl.BlockSpec(memory_space=pltpu.VMEM)] * len(outs),
        compiler_params=pltpu.CompilerParams(vmem_limit_bytes=VMEM_LIMIT),
    )(scalar, *args)


def attend_body(scale, q_ref, kv_ref, column_ref, row_ref, state_ref, out_ref, square_ref):
    rows, width = q_ref.shape[2:]
    across = (((1,), (1,)), ((), ()))
    i, j = (lax.broadcasted_iota(jnp.int32, (DH, DH), axis) for axis in range(2))
    ones = jnp.ones((8, DH), BF16)
    for start in range(0, rows, DH):
        stop = start + DH
        squares = jnp.zeros((8, DH), F32)
        for h in range(width // DH):
            cut = slice(h * DH, (h + 1) * DH)
            q = q_ref[0, 0, start:stop, cut]
            column, row = column_ref[0, h, start:stop], row_ref[0, h, :, :stop]
            raw = lax.dot_general(q, kv_ref[0, 0, :stop, cut], across, preferred_element_type=F32) * scale
            gap = jnp.where(i >= j, column - row[:, start:], -1e30)
            scores = (raw[:, start:] * jnp.exp(gap)).astype(BF16)
            if start:
                border = row[:, start - 1 : start]
                faded = raw[:, :start] * jnp.exp(column - border) * jnp.exp(border - row[:, :start])
                scores = jnp.concatenate([faded.astype(BF16), scores], axis=1)
            intra = jnp.dot(scores, kv_ref[0, 1, :stop, cut], preferred_element_type=F32)
            inter = jnp.dot(jnp.concatenate([q] * 3, axis=1), state_ref[0, h], preferred_element_type=F32)
            attended = intra + inter * (jnp.exp(column) * scale)
            out_ref[0, start:stop, cut] = attended
            for part in split(attended * attended, 2):
                squares += lax.dot_general(ones, part.astype(BF16), across, preferred_element_type=F32)
        square_ref[0, :, start:stop] = squares


def attend(q, kv, column, row, state):
    _, _, rows, width = q.shape
    group = width // DH

    def whole(shape):
        return pl.BlockSpec((1,) + shape, lambda a: (a,) + (0,) * len(shape))

    return pl.pallas_call(
        functools.partial(attend_body, DH**-0.5),
        out_shape=[jax.ShapeDtypeStruct((2, rows, width), F32), jax.ShapeDtypeStruct((2, 8, rows), F32)],
        grid=(2,),
        in_specs=[
            whole((1, rows, width)),
            whole((2, rows, width)),
            whole((group, rows, 1)),
            whole((group, 1, rows)),
            whole((group, 3 * DH, DH)),
        ],
        out_specs=[whole((rows, width)), whole((8, rows))],
        compiler_params=pltpu.CompilerParams(vmem_limit_bytes=VMEM_LIMIT),
        cost_estimate=pl.CostEstimate(flops=4 * 10**9, bytes_accessed=6 * 10**6, transcendentals=10**6),
    )(q, kv, column, row, state)


def on_device(tokens, w_qkv, log_decay, gain):
    rows = tokens.shape[0]
    width = w_qkv.shape[2] // 2
    group = width // DH
    x, z, core = lax.axis_index("x"), lax.axis_index("zl"), lax.axis_index("core")
    place = core.reshape(1)

    def halves(array, axis):
        size = array.shape[axis] // 2
        mine = lax.dynamic_slice_in_dim(array, core * size, size, axis)
        theirs = lax.dynamic_slice_in_dim(array, (1 - core) * size, size, axis)
        return mine, theirs

    kept, sent = halves(w_qkv, 2)
    got = lax.ppermute(sent, "core", SWAP)
    own = jnp.where(core == 0, jnp.concatenate([kept, got], 1), jnp.concatenate([got, kept], 1))
    kept, sent = halves(log_decay, 0)
    decay = jnp.stack([kept, lax.ppermute(tied(sent, own), "core", SWAP)])
    other_tokens = lax.ppermute(tied(tokens, own), "core", SWAP)

    cumulative = jnp.cumsum(decay, axis=2)
    column = cumulative[..., None]
    totals = jnp.broadcast_to(cumulative[:, :, -1][:, :, None, None], (2, group, 1, DH))

    columns = [x, (x + 3) % 4, (x + 1) % 4, (x + 2) % 4]
    index = [[(4 * c + (z + 4 - d) % 4).astype(jnp.int32) for d in range(4)] for c in columns]

    depth = own.shape[1]
    slots = gather_kv(own[1:].reshape(2 * depth, width))
    q_early, q_late = gather_q(own[0])
    early = [(d, n) for d in (0, 1) for n in (0, 1, 2)] + [(0, 3)]
    late = [(d, n) for d in range(4) for n in range(4) if (d, n) not in early]
    kv = None
    for some in (early, late):
        chunk = [index[n][d] for d, n in some]
        kv = project(2, depth, chunk, tokens, other_tokens, [slots[d][n] for d, n in some], kv, some is late)

    shape = (group, DH + TAIL, DH)
    chip, sent, first = small_kernel(state_body, [(shape, F32), (shape, BF16), (shape, F32)], place, kv, column, totals)
    backs = [lax.ppermute(sent, "zl", [(i, (i + j) % 4) for i in range(4)]) for j in (1, 2, 3)]
    before, row = small_kernel(row_body, [(shape, F32), (shape, BF16)], z.reshape(1), chip, *backs)
    backs = [lax.ppermute(row, "x", [(i, i + j) for i in range(4 - j)]) for j in (1, 2, 3)]
    (state,) = small_kernel(incoming_body, [((2, group, 3 * DH, DH), BF16)], place, before, first, *backs)

    q = project(1, depth, sum(index[:3], []), tokens, other_tokens, q_early, None, False)
    q = project(1, depth, index[3], tokens, other_tokens, q_late, q, True)

    attended, squares = attend(q, kv, column, cumulative[:, :, None, :], state)
    squares = squares[:, 0, :]
    summed = squares[0] + lax.ppermute(squares[1], "core", SWAP)
    got = lax.ppermute(attended[1], "core", SWAP)
    summed = summed + sum(lax.ppermute(summed, "y", [(i, (i + j) % 4) for i in range(4)]) for j in (1, 2, 3))
    summed = summed + lax.ppermute(summed, "zh", SWAP)
    scale = lax.rsqrt(summed / (HEAD_COUNT * DH) + 1e-6)[:, None]
    mine = attended[0]
    whole = jnp.where(core == 0, jnp.concatenate([mine, got], 1), jnp.concatenate([got, mine], 1))
    return (whole * scale * gain[None, :]).astype(BF16)


def solution(mesh):
    fine = Mesh(mesh.devices.reshape(4, 4, 2, 4, 2), ("x", "zl", "core", "y", "zh"))
    seq, head = ("x", "zl", "core"), ("y", "zh")
    return jax.shard_map(
        on_device,
        mesh=fine,
        in_specs=(P(seq, None), P(None, seq, head), P(head, seq), P(head)),
        out_specs=P(seq, head),
        check_vma=False,
    )
```

profile of v0, /device:TPU:24, one launch (start us, length us, event | category | flops | bytes accessed | tf_op | source)
XLA Modules:
  0.0 193.1 jit_solution(4131346048231629374)
XLA Ops:
  0.0 1.1 constant_dynamic-slice_fusion.3
  1.2 1.6 collective-permute-done
  2.8 0.3 maximum_select_fusion.1
  3.0 0.2 collective-permute-start.1
  3.3 2.0 %collective-permute-start.14 = (bf16[768,256]{1,0:T(8,128)(2,1)S(1)}, bf16[768,256]{1,0:T(8,128)(2,1)}, u32[]{:S(2)}, u32[]{:S(2)}) collective-permute-start(bf16[768,256]{1,0:T(8,128)(2,1)S(1)} %bitcast.26), channel_id=1, source_target_pairs={{0,16},{16,32},{32,48},{48,0},{1,17},{17,33},{33,49},{49,1},{2,18}... | collective-permute-start | bytes 1179656 | tf_op jit(solution)/shard_map/ppermute | solution.py:29
  5.3 12.5 %collective-permute-done.14.refs_17_ = bf16[768,256]{1,0:T(8,128)(2,1)} collective-permute-done((bf16[768,256]{1,0:T(8,128)(2,1)S(1)}, bf16[768,256]{1,0:T(8,128)(2,1)}, u32[]{:S(2)}, u32[]{:S(2)}) %collective-permute-start.14) | collective-permute-done | bytes 393248 | tf_op jit(solution)/shard_map/ppermute | solution.py:29
  17.8 1.0 collective-permute-start.2
  18.8 1.5 collective-permute-start.9
  20.3 14.5 %collective-permute-done.2 = bf16[384,256]{1,0:T(8,128)(2,1)S(1)} collective-permute-done((bf16[384,256]{1,0:T(8,128)(2,1)S(1)}, bf16[384,256]{1,0:T(8,128)(2,1)S(1)}, u32[]{:S(2)}, u32[]{:S(2)}) %collective-permute-start.2) | collective-permute-done | bytes 196640 | tf_op jit(solution)/shard_map/ppermute | solution.py:42
  34.9 9.5 %collective-permute-done.3 = bf16[384,256]{1,0:T(8,128)(2,1)S(1)} collective-permute-done((bf16[384,256]{1,0:T(8,128)(2,1)S(1)}, bf16[384,256]{1,0:T(8,128)(2,1)S(1)}, u32[]{:S(2)}, u32[]{:S(2)}) %collective-permute-start.3) | collective-permute-done | bytes 196640 | tf_op jit(solution)/shard_map/ppermute | solution.py:42
  44.4 2.8 %collective-permute-start.11 = (bf16[768,256]{1,0:T(8,128)(2,1)S(1)}, bf16[768,256]{1,0:T(8,128)(2,1)}, u32[]{:S(2)}, u32[]{:S(2)}) collective-permute-start(bf16[768,256]{1,0:T(8,128)(2,1)S(1)} %bitcast.28), channel_id=1, source_target_pairs={{0,192},{64,0},{128,64},{192,128},{1,193},{65,1},{129,65},{193,129... | collective-permute-start | bytes 1179656 | tf_op jit(solution)/shard_map/ppermute | solution.py:30
  47.3 7.6 %collective-permute-done.4 = bf16[384,256]{1,0:T(8,128)(2,1)S(1)} collective-permute-done((bf16[384,256]{1,0:T(8,128)(2,1)S(1)}, bf16[384,256]{1,0:T(8,128)(2,1)S(1)}, u32[]{:S(2)}, u32[]{:S(2)}) %collective-permute-start.4) | collective-permute-done | bytes 196640 | tf_op jit(solution)/shard_map/ppermute | solution.py:42
  55.0 1.5 collective-permute-start.10
  56.5 1.6 collective-permute-start.20
  58.1 1.3 collective-permute-start.5
  59.4 2.0 %collective-permute-start.7 = (bf16[1536,256]{1,0:T(8,128)(2,1)S(1)}, bf16[1536,256]{1,0:T(8,128)(2,1)S(1)}, u32[]{:S(2)}, u32[]{:S(2)}) collective-permute-start(bf16[1536,256]{1,0:T(8,128)(2,1)S(1)} %pad_maximum_fusion.refs_24_), channel_id=1, source_target_pairs={{0,192},{64,0},{128,64},{192,128},{1,193},{65,1},{129,65},{193,129... | collective-permute-start | bytes 2359304 | tf_op jit(solution)/shard_map/ppermute | solution.py:45
  61.4 0.9 slice.70
  62.4 1.8 collective-permute-done.10
  64.1 1.5 collective-permute-start.12
  65.7 15.5 %collective-permute-done.12 = bf16[384,256]{1,0:T(8,128)(2,1)} collective-permute-done((bf16[384,256]{1,0:T(8,128)(2,1)S(1)}, bf16[384,256]{1,0:T(8,128)(2,1)}, u32[]{:S(2)}, u32[]{:S(2)}) %collective-permute-start.12) | collective-permute-done | bytes 196640 | tf_op jit(solution)/shard_map/ppermute | solution.py:34
  81.2 2.5 %collective-permute-start.21 = (bf16[768,256]{1,0:T(8,128)(2,1)}, bf16[768,256]{1,0:T(8,128)(2,1)}, u32[]{:S(2)}, u32[]{:S(2)}) collective-permute-start(bf16[768,256]{1,0:T(8,128)(2,1)} %collective-permute-done.19.refs_23_), channel_id=1, source_target_pairs={{0,192},{64,0},{128,64},{192,128},{1,193},{65,1},{129,65},{193,129... | collective-permute-start | bytes 1179656 | tf_op jit(solution)/shard_map/ppermute | solution.py:30
  84.0 0.6 stack.105
  84.6 0.6 stack.106
  85.2 1.4 pad_maximum_fusion.2
  86.6 3.1 %reduce-window.6 = f32[2,2,5,128]{3,2,1,0:T(8,128)} reduce-window(f32[2,2,5,128]{3,2,1,0:T(8,128)} %pad_maximum_fusion.2, f32[]{:T(128)} %constant.98.clone.1), window={size=1x1x1x128 pad=0_0x0_0x0_0x127_0}, to_apply=%region_0.1 | reduce-window | flops 325120 | bytes 20484 | tf_op jit(solution)/shard_map/reduce-window
  89.7 1.6 constant_dynamic-update-slice_fusion.1
  91.3 1.6 constant_dynamic-update-slice_fusion.refs_20_
  92.9 1.5 slice_reduce_fusion
  94.4 1.5 reduce-window.9
  95.9 0.7 slice.71
  96.6 1.6 slice.72
  98.2 0.8 copy-done.9
  99.0 3.2 %collective-permute-start.25 = (bf16[768,256]{1,0:T(8,128)(2,1)}, bf16[768,256]{1,0:T(8,128)(2,1)}, u32[]{:S(2)}, u32[]{:S(2)}) collective-permute-start(bf16[768,256]{1,0:T(8,128)(2,1)} %collective-permute-done.14.refs_17_), channel_id=1, source_target_pairs={{0,192},{64,0},{128,64},{192,128},{1,193},{65,1},{129,65},{193,129... | collective-permute-start | bytes 1179656 | tf_op jit(solution)/shard_map/ppermute | solution.py:30
  102.2 3.2 %collective-permute-start.23 = (bf16[384,256]{1,0:T(8,128)(2,1)}, bf16[384,256]{1,0:T(8,128)(2,1)}, u32[]{:S(2)}, u32[]{:S(2)}) collective-permute-start(bf16[384,256]{1,0:T(8,128)(2,1)} %slice.72), channel_id=1, source_target_pairs={{0,192},{64,0},{128,64},{192,128},{1,193},{65,1},{129,65},{193,129... | collective-permute-start | bytes 589832 | tf_op jit(solution)/shard_map/ppermute | solution.py:34
  105.4 0.8 broadcast_add_fusion
  106.2 1.1 reduce_window_sum.39.column_ref
  107.6 1.1 slice.67
  108.8 2.2 %collective-permute-done.22 = bf16[384,256]{1,0:T(8,128)(2,1)S(1)} collective-permute-done((bf16[384,256]{1,0:T(8,128)(2,1)}, bf16[384,256]{1,0:T(8,128)(2,1)S(1)}, u32[]{:S(2)}, u32[]{:S(2)}) %collective-permute-start.22) | collective-permute-done | bytes 196640 | tf_op jit(solution)/shard_map/ppermute | solution.py:34
  111.0 1.1 collective-permute-start.17
  112.1 2.8 %collective-permute-done.23 = bf16[384,256]{1,0:T(8,128)(2,1)} collective-permute-done((bf16[384,256]{1,0:T(8,128)(2,1)}, bf16[384,256]{1,0:T(8,128)(2,1)}, u32[]{:S(2)}, u32[]{:S(2)}) %collective-permute-start.23) | collective-permute-done | bytes 196640 | tf_op jit(solution)/shard_map/ppermute | solution.py:34
  114.9 1.0 pad_maximum_fusion.1.refs_26_
  115.9 4.0 %collective-permute-start.8 = (bf16[768,256]{1,0:T(8,128)(2,1)S(1)}, bf16[768,256]{1,0:T(8,128)(2,1)S(1)}, u32[]{:S(2)}, u32[]{:S(2)}) collective-permute-start(bf16[768,256]{1,0:T(8,128)(2,1)S(1)} %slice.67), channel_id=1, source_target_pairs={{0,192},{64,0},{128,64},{192,128},{1,193},{65,1},{129,65},{193,129... | collective-permute-start | bytes 1179656 | tf_op jit(solution)/shard_map/ppermute | solution.py:46
  119.9 8.1 %shard_map.48.refs_27_ = f32[2,2,640,256]{3,2,1,0:T(8,128)S(1)} custom-call(s32[7]{0:T(128)S(1)} %stack.104.index_ref, bf16[640,6144]{1,0:T(8,128)(2,1)} %refs_8_.3, bf16[640,6144]{1,0:T(8,128)(2,1)} %refs_8_.3, bf16[640,6144]{1,0:T(8,128)(2,1)} %refs_8_.3, bf16[640,6144]{1,0:T(8,128)(2,1)} %refs_8_.3, bf16[640,6144]{1,0:T(8,128)(2,1)} %refs_8_.3, ...), custom_call_target="tpu_custom_call" | custom-call | flops 3523215360 | bytes 6881280 | tf_op jit(solution)/shard_map/pallas_call | solution.py:73
  128.0 1.6 copy-done
  129.6 9.6 %shard_map.49.kv_ref = bf16[2,2,640,256]{3,2,1,0:T(8,128)(2,1)S(1)} custom-call(s32[9]{0:T(128)S(1)} %stack.103.index_ref, bf16[640,6144]{1,0:T(8,128)(2,1)} %refs_8_.3, bf16[640,6144]{1,0:T(8,128)(2,1)} %refs_8_.3, bf16[640,6144]{1,0:T(8,128)(2,1)} %refs_8_.3, bf16[640,6144]{1,0:T(8,128)(2,1)} %refs_8_.3, bf16[640,6144]{1,0:T(8,128)(2,1)} %refs_8_.3, ...), custom_call_target="tpu_custom_call" | custom-call | flops 4529848320 | bytes 8847360 | tf_op jit(solution)/shard_map/pallas_call | solution.py:73
  139.3 0.8 shard_map.50
  140.2 0.3 collective-permute-start.27
  140.4 4.2 %collective-permute-start.28 = (bf16[2,144,128]{2,1,0:T(8,128)(2,1)S(1)}, bf16[2,144,128]{2,1,0:T(8,128)(2,1)S(1)}, u32[]{:S(2)}, u32[]{:S(2)}) collective-permute-start(bf16[2,144,128]{2,1,0:T(8,128)(2,1)S(1)} %get-tuple-element.17), channel_id=1, source_target_pairs={{0,32},{16,48},{32,0},{48,16},{1,33},{17,49},{33,1},{49,17},{2,34}... | collective-permute-start | bytes 221192 | tf_op jit(solution)/shard_map/ppermute | solution.py:266
  144.6 2.6 %collective-permute-start.29 = (bf16[2,144,128]{2,1,0:T(8,128)(2,1)S(1)}, bf16[2,144,128]{2,1,0:T(8,128)(2,1)S(1)}, u32[]{:S(2)}, u32[]{:S(2)}) collective-permute-start(bf16[2,144,128]{2,1,0:T(8,128)(2,1)S(1)} %get-tuple-element.17), channel_id=1, source_target_pairs={{0,48},{16,0},{32,16},{48,32},{1,49},{17,1},{33,17},{49,33},{2,50}... | collective-permute-start | bytes 221192 | tf_op jit(solution)/shard_map/ppermute | solution.py:266
  147.3 8.2 %shard_map.46.refs_10_ = f32[2,1,640,256]{3,2,1,0:T(8,128)S(1)} custom-call(s32[12]{0:T(128)S(1)} %stack.102.index_ref, bf16[640,6144]{1,0:T(8,128)(2,1)} %refs_8_.3, bf16[640,6144]{1,0:T(8,128)(2,1)} %refs_8_.3, bf16[640,6144]{1,0:T(8,128)(2,1)} %refs_8_.3, bf16[640,6144]{1,0:T(8,128)(2,1)} %refs_8_.3, bf16[640,6144]{1,0:T(8,128)(2,1)} %refs_8_.3, ...), custom_call_target="tpu_custom_call" | custom-call | flops 3019898880 | bytes 11796480 | tf_op jit(solution)/shard_map/pallas_call | solution.py:73
  155.7 1.3 collective-permute-start.30
  157.0 5.7 %collective-permute-start.31 = (bf16[2,144,128]{2,1,0:T(8,128)(2,1)S(1)}, bf16[2,144,128]{2,1,0:T(8,128)(2,1)S(1)}, u32[]{:S(2)}, u32[]{:S(2)}) collective-permute-start(bf16[2,144,128]{2,1,0:T(8,128)(2,1)S(1)} %get-tuple-element.20), channel_id=1, source_target_pairs={{0,128},{64,192},{1,129},{65,193},{2,130},{66,194},{3,131},{67,195... | collective-permute-start | bytes 221192 | tf_op jit(solution)/shard_map/ppermute | solution.py:268
  162.7 1.3 collective-permute-start.32
  164.0 4.7 %shard_map.47.q_ref = bf16[2,1,640,256]{3,2,1,0:T(8,128)(2,1)S(1)} custom-call(s32[4]{0:T(128)S(1)} %pad_add_fusion.index_ref, bf16[640,6144]{1,0:T(8,128)(2,1)} %refs_8_.3, bf16[640,6144]{1,0:T(8,128)(2,1)} %refs_8_.3, bf16[640,6144]{1,0:T(8,128)(2,1)} %refs_8_.3, bf16[640,6144]{1,0:T(8,128)(2,1)} %refs_8_.3, ...), custom_call_target="tpu_custom_call" | custom-call | flops 1006632960 | bytes 3932160 | tf_op jit(solution)/shard_map/pallas_call | solution.py:73
  168.9 5.7 %shard_map.53 = (f32[2,640,256]{2,1,0:T(8,128)S(1)}, f32[2,8,640]{2,1,0:T(8,128)S(1)}) custom-call(bf16[2,1,640,256]{3,2,1,0:T(8,128)(2,1)S(1)} %shard_map.47.q_ref, bf16[2,2,640,256]{3,2,1,0:T(8,128)(2,1)S(1)} %shard_map.49.kv_ref, f32[2,2,640,1]{3,2,1,0:T(8,128)S(1)} %reduce_window_sum.39.column_ref, f32[2,2,1,640]{3,2,1,0:T(1,128)S(1)} %reduce_window_sum.40.row_ref, ...), custom_call_target="tpu_custom_call" | custom-call | flops 4000000000 | bytes 6000000 | tf_op jit(solution)/shard_map/pallas_call | solution.py:210
  174.8 0.6 collective-permute-start.34
  175.4 1.5 collective-permute-done.34
  177.1 2.6 %collective-permute-start.36 = (f32[640]{0:T(1024)S(1)}, f32[640]{0:T(1024)S(1)}, u32[]{:S(2)}, u32[]{:S(2)}) collective-permute-start(f32[640]{0:T(1024)S(1)} %add.182), channel_id=1, source_target_pairs={{0,4},{2,6},{4,0},{6,2},{1,5},{3,7},{5,1},{7,3},{8,12},{10,14},{12... | collective-permute-start | bytes 7688 | tf_op jit(solution)/shard_map/ppermute | solution.py:278
  179.7 0.8 collective-permute-done.35
  180.5 1.7 collective-permute-done.36
  182.2 2.3 %collective-permute-done.37 = f32[640]{0:T(1024)S(1)} collective-permute-done((f32[640]{0:T(1024)S(1)}, f32[640]{0:T(1024)S(1)}, u32[]{:S(2)}, u32[]{:S(2)}) %collective-permute-start.37) | collective-permute-done | bytes 2592 | tf_op jit(solution)/shard_map/ppermute | solution.py:278
  184.5 5.0 %collective-permute-start.38 = (f32[640]{0:T(1024)S(1)}, f32[640]{0:T(1024)S(1)}, u32[]{:S(2)}, u32[]{:S(2)}) collective-permute-start(f32[640]{0:T(1024)S(1)} %add_add_fusion), channel_id=1, source_target_pairs={{0,1},{1,0},{2,3},{3,2},{4,5},{5,4},{6,7},{7,6},{8,9},{9,8},{10,11... | collective-permute-start | bytes 7688 | tf_op jit(solution)/shard_map/ppermute | solution.py:279
  189.6 2.5 %collective-permute-done.38 = f32[640]{0:T(1024)S(1)} collective-permute-done((f32[640]{0:T(1024)S(1)}, f32[640]{0:T(1024)S(1)}, u32[]{:S(2)}, u32[]{:S(2)}) %collective-permute-start.38) | collective-permute-done | bytes 2592 | tf_op jit(solution)/shard_map/ppermute | solution.py:279
  192.1 1.0 fusion.2
  (85 shorter events, 2.0 us)
Async XLA Ops:
  1.1 46.1 %copy-start.11 = (f32[4,640]{1,0:T(4,128)S(1)}, f32[4,640]{1,0:T(4,128)}, u32[]{:S(2)}) copy-start(f32[4,640]{1,0:T(4,128)} %param.6) | copy-start | bytes 30724
  1.1 1.7 collective-permute-start
  3.0 112.9 %collective-permute-start.1 = (bf16[640,6144]{1,0:T(8,128)(2,1)}, bf16[640,6144]{1,0:T(8,128)(2,1)}, u32[]{:S(2)}, u32[]{:S(2)}) collective-permute-start(bf16[640,6144]{1,0:T(8,128)(2,1)} %refs_8_.3), channel_id=1, source_target_pairs={{0,8},{8,0},{1,9},{9,1},{2,10},{10,2},{3,11},{11,3},{4,12},{12,4},... | collective-permute-start | bytes 23592968 | tf_op jit(solution)/shard_map/ppermute | solution.py:245
  3.3 14.5 %collective-permute-start.14 = (bf16[768,256]{1,0:T(8,128)(2,1)S(1)}, bf16[768,256]{1,0:T(8,128)(2,1)}, u32[]{:S(2)}, u32[]{:S(2)}) collective-permute-start(bf16[768,256]{1,0:T(8,128)(2,1)S(1)} %bitcast.26), channel_id=1, source_target_pairs={{0,16},{16,32},{32,48},{48,0},{1,17},{17,33},{33,49},{49,1},{2,18}... | collective-permute-start | bytes 1179656 | tf_op jit(solution)/shard_map/ppermute | solution.py:29
  17.8 17.0 %collective-permute-start.15 = (bf16[768,256]{1,0:T(8,128)(2,1)}, bf16[768,256]{1,0:T(8,128)(2,1)S(1)}, u32[]{:S(2)}, u32[]{:S(2)}) collective-permute-start(bf16[768,256]{1,0:T(8,128)(2,1)} %collective-permute-done.14.refs_17_), channel_id=1, source_target_pairs={{0,16},{16,32},{32,48},{48,0},{1,17},{17,33},{33,49},{49,1},{2,18}... | collective-permute-start | bytes 1179656 | tf_op jit(solution)/shard_map/ppermute | solution.py:29
  17.8 17.0 %collective-permute-start.2 = (bf16[384,256]{1,0:T(8,128)(2,1)S(1)}, bf16[384,256]{1,0:T(8,128)(2,1)S(1)}, u32[]{:S(2)}, u32[]{:S(2)}) collective-permute-start(bf16[384,256]{1,0:T(8,128)(2,1)S(1)} %slice_bitcast_fusion.2), channel_id=1, source_target_pairs={{0,16},{16,32},{32,48},{48,0},{1,17},{17,33},{33,49},{49,1},{2,18}... | collective-permute-start | bytes 589832 | tf_op jit(solution)/shard_map/ppermute | solution.py:42
  18.8 28.4 %collective-permute-start.9 = (bf16[768,256]{1,0:T(8,128)(2,1)S(1)}, bf16[768,256]{1,0:T(8,128)(2,1)S(1)}, u32[]{:S(2)}, u32[]{:S(2)}) collective-permute-start(bf16[768,256]{1,0:T(8,128)(2,1)S(1)} %bitcast.27), channel_id=1, source_target_pairs={{0,64},{64,128},{128,192},{192,0},{1,65},{65,129},{129,193},{193,1... | collective-permute-start | bytes 1179656 | tf_op jit(solution)/shard_map/ppermute | solution.py:30
  34.8 9.6 %collective-permute-start.3 = (bf16[384,256]{1,0:T(8,128)(2,1)S(1)}, bf16[384,256]{1,0:T(8,128)(2,1)S(1)}, u32[]{:S(2)}, u32[]{:S(2)}) collective-permute-start(bf16[384,256]{1,0:T(8,128)(2,1)S(1)} %collective-permute-done.2), channel_id=1, source_target_pairs={{0,16},{16,32},{32,48},{48,0},{1,17},{17,33},{33,49},{49,1},{2,18}... | collective-permute-start | bytes 589832 | tf_op jit(solution)/shard_map/ppermute | solution.py:42
  34.8 21.7 %copy-start.7 = (bf16[768,256]{1,0:T(8,128)(2,1)}, bf16[768,256]{1,0:T(8,128)(2,1)S(1)}, u32[]{:S(2)}) copy-start(bf16[768,256]{1,0:T(8,128)(2,1)S(1)} %collective-permute-done.15.refs_19_) | copy-start | bytes 1179652
  34.8 21.6 %collective-permute-start.19 = (bf16[768,256]{1,0:T(8,128)(2,1)S(1)}, bf16[768,256]{1,0:T(8,128)(2,1)}, u32[]{:S(2)}, u32[]{:S(2)}) collective-permute-start(bf16[768,256]{1,0:T(8,128)(2,1)S(1)} %collective-permute-done.15.refs_19_), channel_id=1, source_target_pairs={{0,16},{16,32},{32,48},{48,0},{1,17},{17,33},{33,49},{49,1},{2,18}... | collective-permute-start | bytes 1179656 | tf_op jit(solution)/shard_map/ppermute | solution.py:29
  44.4 10.5 %collective-permute-start.4 = (bf16[384,256]{1,0:T(8,128)(2,1)S(1)}, bf16[384,256]{1,0:T(8,128)(2,1)S(1)}, u32[]{:S(2)}, u32[]{:S(2)}) collective-permute-start(bf16[384,256]{1,0:T(8,128)(2,1)S(1)} %collective-permute-done.3), channel_id=1, source_target_pairs={{0,16},{16,32},{32,48},{48,0},{1,17},{17,33},{33,49},{49,1},{2,18}... | collective-permute-start | bytes 589832 | tf_op jit(solution)/shard_map/ppermute | solution.py:42
  44.4 14.9 %collective-permute-start.11 = (bf16[768,256]{1,0:T(8,128)(2,1)S(1)}, bf16[768,256]{1,0:T(8,128)(2,1)}, u32[]{:S(2)}, u32[]{:S(2)}) collective-permute-start(bf16[768,256]{1,0:T(8,128)(2,1)S(1)} %bitcast.28), channel_id=1, source_target_pairs={{0,192},{64,0},{128,64},{192,128},{1,193},{65,1},{129,65},{193,129... | collective-permute-start | bytes 1179656 | tf_op jit(solution)/shard_map/ppermute | solution.py:30
  47.2 9.2 %copy-start.5 = (bf16[768,256]{1,0:T(8,128)(2,1)}, bf16[768,256]{1,0:T(8,128)(2,1)S(1)}, u32[]{:S(2)}) copy-start(bf16[768,256]{1,0:T(8,128)(2,1)S(1)} %collective-permute-done.9.refs_15_) | copy-start | bytes 1179652
  47.2 10.9 %collective-permute-start.26 = (f32[2,640]{1,0:T(2,128)S(1)}, f32[2,640]{1,0:T(2,128)S(1)}, u32[]{:S(2)}, u32[]{:S(2)}) collective-permute-start(f32[2,640]{1,0:T(2,128)S(1)} %get-tuple-element.15), channel_id=1, source_target_pairs={{0,8},{8,0},{1,9},{9,1},{2,10},{10,2},{3,11},{11,3},{4,12},{12,4},... | collective-permute-start | bytes 15368 | tf_op jit(solution)/shard_map/ppermute | solution.py:244
  55.0 9.2 %collective-permute-start.10 = (bf16[384,256]{1,0:T(8,128)(2,1)S(1)}, bf16[384,256]{1,0:T(8,128)(2,1)}, u32[]{:S(2)}, u32[]{:S(2)}) collective-permute-start(bf16[384,256]{1,0:T(8,128)(2,1)S(1)} %slice.69), channel_id=1, source_target_pairs={{0,64},{64,128},{128,192},{192,0},{1,65},{65,129},{129,193},{193,1... | collective-permute-start | bytes 589832 | tf_op jit(solution)/shard_map/ppermute | solution.py:34
  56.5 28.7 %collective-permute-start.20 = (bf16[768,256]{1,0:T(8,128)(2,1)}, bf16[768,256]{1,0:T(8,128)(2,1)S(1)}, u32[]{:S(2)}, u32[]{:S(2)}) collective-permute-start(bf16[768,256]{1,0:T(8,128)(2,1)} %collective-permute-done.19.refs_23_), channel_id=1, source_target_pairs={{0,64},{64,128},{128,192},{192,0},{1,65},{65,129},{129,193},{193,1... | collective-permute-start | bytes 1179656 | tf_op jit(solution)/shard_map/ppermute | solution.py:30
  58.1 44.1 %collective-permute-start.5 = (bf16[1536,256]{1,0:T(8,128)(2,1)S(1)}, bf16[1536,256]{1,0:T(8,128)(2,1)S(1)}, u32[]{:S(2)}, u32[]{:S(2)}) collective-permute-start(bf16[1536,256]{1,0:T(8,128)(2,1)S(1)} %pad_maximum_fusion.refs_24_), channel_id=1, source_target_pairs={{0,64},{64,128},{128,192},{192,0},{1,65},{65,129},{129,193},{193,1... | collective-permute-start | bytes 2359304 | tf_op jit(solution)/shard_map/ppermute | solution.py:45
  59.4 42.8 %collective-permute-start.7 = (bf16[1536,256]{1,0:T(8,128)(2,1)S(1)}, bf16[1536,256]{1,0:T(8,128)(2,1)S(1)}, u32[]{:S(2)}, u32[]{:S(2)}) collective-permute-start(bf16[1536,256]{1,0:T(8,128)(2,1)S(1)} %pad_maximum_fusion.refs_24_), channel_id=1, source_target_pairs={{0,192},{64,0},{128,64},{192,128},{1,193},{65,1},{129,65},{193,129... | collective-permute-start | bytes 2359304 | tf_op jit(solution)/shard_map/ppermute | solution.py:45
  64.1 17.1 %collective-permute-start.12 = (bf16[384,256]{1,0:T(8,128)(2,1)S(1)}, bf16[384,256]{1,0:T(8,128)(2,1)}, u32[]{:S(2)}, u32[]{:S(2)}) collective-permute-start(bf16[384,256]{1,0:T(8,128)(2,1)S(1)} %slice.70), channel_id=1, source_target_pairs={{0,192},{64,0},{128,64},{192,128},{1,193},{65,1},{129,65},{193,129... | collective-permute-start | bytes 589832 | tf_op jit(solution)/shard_map/ppermute | solution.py:34
  81.2 11.8 %collective-permute-start.21 = (bf16[768,256]{1,0:T(8,128)(2,1)}, bf16[768,256]{1,0:T(8,128)(2,1)}, u32[]{:S(2)}, u32[]{:S(2)}) collective-permute-start(bf16[768,256]{1,0:T(8,128)(2,1)} %collective-permute-done.19.refs_23_), channel_id=1, source_target_pairs={{0,192},{64,0},{128,64},{192,128},{1,193},{65,1},{129,65},{193,129... | collective-permute-start | bytes 1179656 | tf_op jit(solution)/shard_map/ppermute | solution.py:30
  85.2 20.2 %copy-start.3 = (bf16[768,256]{1,0:T(8,128)(2,1)}, bf16[768,256]{1,0:T(8,128)(2,1)S(1)}, u32[]{:S(2)}) copy-start(bf16[768,256]{1,0:T(8,128)(2,1)S(1)} %collective-permute-done.20.refs_24_) | copy-start | bytes 1179652
  85.2 13.0 %collective-permute-start.24 = (bf16[768,256]{1,0:T(8,128)(2,1)}, bf16[768,256]{1,0:T(8,128)(2,1)S(1)}, u32[]{:S(2)}, u32[]{:S(2)}) collective-permute-start(bf16[768,256]{1,0:T(8,128)(2,1)} %collective-permute-done.14.refs_17_), channel_id=1, source_target_pairs={{0,64},{64,128},{128,192},{192,0},{1,65},{65,129},{129,193},{193,1... | collective-permute-start | bytes 1179656 | tf_op jit(solution)/shard_map/ppermute | solution.py:30
  92.9 15.8 %collective-permute-start.13 = (bf16[768,256]{1,0:T(8,128)(2,1)}, bf16[768,256]{1,0:T(8,128)(2,1)}, u32[]{:S(2)}, u32[]{:S(2)}) collective-permute-start(bf16[768,256]{1,0:T(8,128)(2,1)} %constant_dynamic-update-slice_fusion.refs_20_), channel_id=1, source_target_pairs={{0,16},{16,32},{32,48},{48,0},{1,17},{17,33},{33,49},{49,1},{2,18}... | collective-permute-start | bytes 1179656 | tf_op jit(solution)/shard_map/ppermute | solution.py:32
  98.2 0.8 copy-start.9
  99.0 16.9 %collective-permute-start.25 = (bf16[768,256]{1,0:T(8,128)(2,1)}, bf16[768,256]{1,0:T(8,128)(2,1)}, u32[]{:S(2)}, u32[]{:S(2)}) collective-permute-start(bf16[768,256]{1,0:T(8,128)(2,1)} %collective-permute-done.14.refs_17_), channel_id=1, source_target_pairs={{0,192},{64,0},{128,64},{192,128},{1,193},{65,1},{129,65},{193,129... | collective-permute-start | bytes 1179656 | tf_op jit(solution)/shard_map/ppermute | solution.py:30
  102.1 8.9 %collective-permute-start.22 = (bf16[384,256]{1,0:T(8,128)(2,1)}, bf16[384,256]{1,0:T(8,128)(2,1)S(1)}, u32[]{:S(2)}, u32[]{:S(2)}) collective-permute-start(bf16[384,256]{1,0:T(8,128)(2,1)} %slice.71), channel_id=1, source_target_pairs={{0,64},{64,128},{128,192},{192,0},{1,65},{65,129},{129,193},{193,1... | collective-permute-start | bytes 589832 | tf_op jit(solution)/shard_map/ppermute | solution.py:34
  102.2 3.2 %copy-start.1 = (bf16[1536,256]{1,0:T(8,128)(2,1)}, bf16[1536,256]{1,0:T(8,128)(2,1)S(1)}, u32[]{:S(2)}) copy-start(bf16[1536,256]{1,0:T(8,128)(2,1)S(1)} %collective-permute-done.7.refs_26_) | copy-start | bytes 2359300
  102.2 12.7 %collective-permute-start.23 = (bf16[384,256]{1,0:T(8,128)(2,1)}, bf16[384,256]{1,0:T(8,128)(2,1)}, u32[]{:S(2)}, u32[]{:S(2)}) collective-permute-start(bf16[384,256]{1,0:T(8,128)(2,1)} %slice.72), channel_id=1, source_target_pairs={{0,192},{64,0},{128,64},{192,128},{1,193},{65,1},{129,65},{193,129... | collective-permute-start | bytes 589832 | tf_op jit(solution)/shard_map/ppermute | solution.py:34
  107.4 1.4 copy-start.8
  107.4 12.6 %copy-start.6 = (bf16[768,256]{1,0:T(8,128)(2,1)S(1)}, bf16[768,256]{1,0:T(8,128)(2,1)}, u32[]{:S(2)}) copy-start(bf16[768,256]{1,0:T(8,128)(2,1)} %copy-done.5) | copy-start | bytes 1179652
  107.4 12.5 %copy-start.10 = (bf16[768,256]{1,0:T(8,128)(2,1)S(1)}, bf16[768,256]{1,0:T(8,128)(2,1)}, u32[]{:S(2)}) copy-start(bf16[768,256]{1,0:T(8,128)(2,1)} %copy-done.9) | copy-start | bytes 1179652
  108.7 20.8 %collective-permute-start.16 = (bf16[768,256]{1,0:T(8,128)(2,1)S(1)}, bf16[768,256]{1,0:T(8,128)(2,1)S(1)}, u32[]{:S(2)}, u32[]{:S(2)}) collective-permute-start(bf16[768,256]{1,0:T(8,128)(2,1)S(1)} %copy-done.8), channel_id=1, source_target_pairs={{0,64},{64,128},{128,192},{192,0},{1,65},{65,129},{129,193},{193,1... | collective-permute-start | bytes 1179656 | tf_op jit(solution)/shard_map/ppermute | solution.py:30
  111.0 18.6 %collective-permute-start.17 = (bf16[768,256]{1,0:T(8,128)(2,1)S(1)}, bf16[768,256]{1,0:T(8,128)(2,1)S(1)}, u32[]{:S(2)}, u32[]{:S(2)}) collective-permute-start(bf16[768,256]{1,0:T(8,128)(2,1)S(1)} %copy-done.8), channel_id=1, source_target_pairs={{0,192},{64,0},{128,64},{192,128},{1,193},{65,1},{129,65},{193,129... | collective-permute-start | bytes 1179656 | tf_op jit(solution)/shard_map/ppermute | solution.py:30
  114.9 14.7 %collective-permute-start.18 = (bf16[768,256]{1,0:T(8,128)(2,1)}, bf16[768,256]{1,0:T(8,128)(2,1)S(1)}, u32[]{:S(2)}, u32[]{:S(2)}) collective-permute-start(bf16[768,256]{1,0:T(8,128)(2,1)} %collective-permute-done.13.refs_18_), channel_id=1, source_target_pairs={{0,16},{16,32},{32,48},{48,0},{1,17},{17,33},{33,49},{49,1},{2,18}... | collective-permute-start | bytes 1179656 | tf_op jit(solution)/shard_map/ppermute | solution.py:32
  115.8 13.8 %copy-start.4 = (bf16[768,256]{1,0:T(8,128)(2,1)S(1)}, bf16[768,256]{1,0:T(8,128)(2,1)}, u32[]{:S(2)}) copy-start(bf16[768,256]{1,0:T(8,128)(2,1)} %copy-done.3) | copy-start | bytes 1179652
  115.8 48.2 %collective-permute-start.6 = (bf16[768,256]{1,0:T(8,128)(2,1)S(1)}, bf16[768,256]{1,0:T(8,128)(2,1)S(1)}, u32[]{:S(2)}, u32[]{:S(2)}) collective-permute-start(bf16[768,256]{1,0:T(8,128)(2,1)S(1)} %slice.66), channel_id=1, source_target_pairs={{0,64},{64,128},{128,192},{192,0},{1,65},{65,129},{129,193},{193,1... | collective-permute-start | bytes 1179656 | tf_op jit(solution)/shard_map/ppermute | solution.py:46
  115.9 48.1 %collective-permute-start.8 = (bf16[768,256]{1,0:T(8,128)(2,1)S(1)}, bf16[768,256]{1,0:T(8,128)(2,1)S(1)}, u32[]{:S(2)}, u32[]{:S(2)}) collective-permute-start(bf16[768,256]{1,0:T(8,128)(2,1)S(1)} %slice.67), channel_id=1, source_target_pairs={{0,192},{64,0},{128,64},{192,128},{1,193},{65,1},{129,65},{193,129... | collective-permute-start | bytes 1179656 | tf_op jit(solution)/shard_map/ppermute | solution.py:46
  128.0 1.6 copy-start
  139.3 8.0 %copy-start.2 = (bf16[1536,256]{1,0:T(8,128)(2,1)S(1)}, bf16[1536,256]{1,0:T(8,128)(2,1)}, u32[]{:S(2)}) copy-start(bf16[1536,256]{1,0:T(8,128)(2,1)} %copy-done.1) | copy-start | bytes 2359300
  140.2 15.3 %collective-permute-start.27 = (bf16[2,144,128]{2,1,0:T(8,128)(2,1)S(1)}, bf16[2,144,128]{2,1,0:T(8,128)(2,1)S(1)}, u32[]{:S(2)}, u32[]{:S(2)}) collective-permute-start(bf16[2,144,128]{2,1,0:T(8,128)(2,1)S(1)} %get-tuple-element.17), channel_id=1, source_target_pairs={{0,16},{16,32},{32,48},{48,0},{1,17},{17,33},{33,49},{49,1},{2,18}... | collective-permute-start | bytes 221192 | tf_op jit(solution)/shard_map/ppermute | solution.py:266
  140.4 15.1 %collective-permute-start.28 = (bf16[2,144,128]{2,1,0:T(8,128)(2,1)S(1)}, bf16[2,144,128]{2,1,0:T(8,128)(2,1)S(1)}, u32[]{:S(2)}, u32[]{:S(2)}) collective-permute-start(bf16[2,144,128]{2,1,0:T(8,128)(2,1)S(1)} %get-tuple-element.17), channel_id=1, source_target_pairs={{0,32},{16,48},{32,0},{48,16},{1,33},{17,49},{33,1},{49,17},{2,34}... | collective-permute-start | bytes 221192 | tf_op jit(solution)/shard_map/ppermute | solution.py:266
  144.6 10.9 %collective-permute-start.29 = (bf16[2,144,128]{2,1,0:T(8,128)(2,1)S(1)}, bf16[2,144,128]{2,1,0:T(8,128)(2,1)S(1)}, u32[]{:S(2)}, u32[]{:S(2)}) collective-permute-start(bf16[2,144,128]{2,1,0:T(8,128)(2,1)S(1)} %get-tuple-element.17), channel_id=1, source_target_pairs={{0,48},{16,0},{32,16},{48,32},{1,49},{17,1},{33,17},{49,33},{2,50}... | collective-permute-start | bytes 221192 | tf_op jit(solution)/shard_map/ppermute | solution.py:266
  155.7 13.1 %collective-permute-start.30 = (bf16[2,144,128]{2,1,0:T(8,128)(2,1)S(1)}, bf16[2,144,128]{2,1,0:T(8,128)(2,1)S(1)}, u32[]{:S(2)}, u32[]{:S(2)}) collective-permute-start(bf16[2,144,128]{2,1,0:T(8,128)(2,1)S(1)} %get-tuple-element.20), channel_id=1, source_target_pairs={{0,64},{64,128},{128,192},{1,65},{65,129},{129,193},{2,66},{66,130... | collective-permute-start | bytes 221192 | tf_op jit(solution)/shard_map/ppermute | solution.py:268
  157.0 11.8 %collective-permute-start.31 = (bf16[2,144,128]{2,1,0:T(8,128)(2,1)S(1)}, bf16[2,144,128]{2,1,0:T(8,128)(2,1)S(1)}, u32[]{:S(2)}, u32[]{:S(2)}) collective-permute-start(bf16[2,144,128]{2,1,0:T(8,128)(2,1)S(1)} %get-tuple-element.20), channel_id=1, source_target_pairs={{0,128},{64,192},{1,129},{65,193},{2,130},{66,194},{3,131},{67,195... | collective-permute-start | bytes 221192 | tf_op jit(solution)/shard_map/ppermute | solution.py:268
  162.7 6.1 %collective-permute-start.32 = (bf16[2,144,128]{2,1,0:T(8,128)(2,1)S(1)}, bf16[2,144,128]{2,1,0:T(8,128)(2,1)S(1)}, u32[]{:S(2)}, u32[]{:S(2)}) collective-permute-start(bf16[2,144,128]{2,1,0:T(8,128)(2,1)S(1)} %get-tuple-element.20), channel_id=1, source_target_pairs={{0,192},{1,193},{2,194},{3,195},{4,196},{5,197},{6,198},{7,199},{8... | collective-permute-start | bytes 221192 | tf_op jit(solution)/shard_map/ppermute | solution.py:268
  174.6 17.5 %copy-start.12 = (f32[512]{0:T(512)S(1)}, f32[512]{0:T(512)}, u32[]{:S(2)}) copy-start(f32[512]{0:T(512)} %param.7) | copy-start | bytes 6148
  174.7 17.4 %collective-permute-start.33 = (f32[640,256]{1,0:T(8,128)S(1)}, f32[640,256]{1,0:T(8,128)S(1)}, u32[]{:S(2)}, u32[]{:S(2)}) collective-permute-start(f32[640,256]{1,0:T(8,128)S(1)} %get-tuple-element.26), channel_id=1, source_target_pairs={{0,8},{8,0},{1,9},{9,1},{2,10},{10,2},{3,11},{11,3},{4,12},{12,4},... | collective-permute-start | bytes 1966088 | tf_op jit(solution)/shard_map/ppermute | solution.py:277
  174.8 2.1 %collective-permute-start.34 = (f32[640]{0:T(1024)S(1)}, f32[640]{0:T(1024)S(1)}, u32[]{:S(2)}, u32[]{:S(2)}) collective-permute-start(f32[640]{0:T(1024)S(1)} %get-tuple-element.23), channel_id=1, source_target_pairs={{0,8},{8,0},{1,9},{9,1},{2,10},{10,2},{3,11},{11,3},{4,12},{12,4},... | collective-permute-start | bytes 7688 | tf_op jit(solution)/shard_map/ppermute | solution.py:276
  176.9 3.6 %collective-permute-start.35 = (f32[640]{0:T(1024)S(1)}, f32[640]{0:T(1024)S(1)}, u32[]{:S(2)}, u32[]{:S(2)}) collective-permute-start(f32[640]{0:T(1024)S(1)} %add.182), channel_id=1, source_target_pairs={{0,2},{2,4},{4,6},{6,0},{1,3},{3,5},{5,7},{7,1},{8,10},{10,12},{12... | collective-permute-start | bytes 7688 | tf_op jit(solution)/shard_map/ppermute | solution.py:278
  177.1 5.1 %collective-permute-start.36 = (f32[640]{0:T(1024)S(1)}, f32[640]{0:T(1024)S(1)}, u32[]{:S(2)}, u32[]{:S(2)}) collective-permute-start(f32[640]{0:T(1024)S(1)} %add.182), channel_id=1, source_target_pairs={{0,4},{2,6},{4,0},{6,2},{1,5},{3,7},{5,1},{7,3},{8,12},{10,14},{12... | collective-permute-start | bytes 7688 | tf_op jit(solution)/shard_map/ppermute | solution.py:278
  179.7 4.8 %collective-permute-start.37 = (f32[640]{0:T(1024)S(1)}, f32[640]{0:T(1024)S(1)}, u32[]{:S(2)}, u32[]{:S(2)}) collective-permute-start(f32[640]{0:T(1024)S(1)} %add.182), channel_id=1, source_target_pairs={{0,6},{2,0},{4,2},{6,4},{1,7},{3,1},{5,3},{7,5},{8,14},{10,8},{12,... | collective-permute-start | bytes 7688 | tf_op jit(solution)/shard_map/ppermute | solution.py:278
  184.5 7.5 %collective-permute-start.38 = (f32[640]{0:T(1024)S(1)}, f32[640]{0:T(1024)S(1)}, u32[]{:S(2)}, u32[]{:S(2)}) collective-permute-start(f32[640]{0:T(1024)S(1)} %add_add_fusion), channel_id=1, source_target_pairs={{0,1},{1,0},{2,3},{3,2},{4,5},{5,4},{6,7},{7,6},{8,9},{9,8},{10,11... | collective-permute-start | bytes 7688 | tf_op jit(solution)/shard_map/ppermute | solution.py:279
where the time goes:
time: 194 us; the launch traced here: 193 us
  waiting for transfers between devices  76.7 us (40%)
  starting transfers between devices  53.7 us (28%)
  Pallas kernels  37.4 us (19%)
  local copies, waits for them, and re-layouts  15.6 us (8%)
  other arithmetic  9.2 us (5%)
    ppermute x3, waiting for transfers between devices, gather_q(): columns.append(lax.ppermute(columns[-1], 'zl', NEXT))  31.6 us
    pallas_call x4, Pallas kernels, project(): pl.pallas_call(functools.partial(project_body, count, chunks, parts, acc...  30.6 us
    ppermute x2, waiting for transfers between devices, gather_kv(): lax.ppermute(left[half:], 'x', LAST)  18.3 us
    ppermute x8, starting transfers between devices, gather_kv(): right, left = (lax.ppermute(own, 'x', NEXT), lax.ppermute(own, 'x', LAST))  12.6 us
    ppermute x3, waiting for transfers between devices, gather_kv(): own = lax.ppermute(own, 'zl', NEXT)  12.5 us
    ppermute x3, starting transfers between devices, on_device(): lax.ppermute(row, 'x', [(i, i + j) for i in range(4 - j)])  8.28 us
    ppermute x3, starting transfers between devices, on_device(): lax.ppermute(sent, 'zl', [(i, (i + j) % 4) for i in range(4)])  7.11 us
    pallas_call x1, Pallas kernels, attend(): pl.pallas_call(functools.partial(attend_body, DH ** (-0.5)), out_shape=[j...  5.66 us
  transfers between devices with their start and end apart: 39, of which 14 were waited for; matrix products, arithmetic and copies ran while one was open for 10% of the time, Pallas kernels for 16%

commit v1 on v0

--- a/solution.py
+++ b/solution.py
@@ -17,45 +17,22 @@
 VMEM_LIMIT = 48 * 1024 * 1024
 
 
+ACROSS = (((1,), (1,)), ((), ()))
+
+
 def tied(value, *others):
     return lax.optimization_barrier((value, others))[0]
 
 
-def gather_kv(own):
-    half = own.shape[0] // 2
-    slots, opposite = [], None
-    for distance in range(4):
-        if distance:
-            own = lax.ppermute(own, "zl", NEXT)
-        right, left = lax.ppermute(own, "x", NEXT), lax.ppermute(own, "x", LAST)
-        if distance in (1, 2):
-            opposite = lax.ppermute(opposite, "zl", NEXT)
-        else:
-            opposite = jnp.concatenate([lax.ppermute(right[:half], "x", NEXT), lax.ppermute(left[half:], "x", LAST)])
-        slots.append((own, right, left, opposite))
-    return slots
-
-
-def gather_q(own):
-    columns = [own]
-    for _ in range(3):
-        columns.append(lax.ppermute(columns[-1], "zl", NEXT))
-    column = jnp.concatenate(columns)
-    half = column.shape[0] // 2
-    right, left = lax.ppermute(column, "x", NEXT), lax.ppermute(column, "x", LAST)
-    return [column, right, left], [lax.ppermute(right[:half], "x", NEXT), lax.ppermute(left[half:], "x", LAST)]
-
-
-def project_body(count, chunks, parts, has_acc, index_ref, *refs):
-    mine, theirs, weights = refs[:chunks], refs[chunks : 2 * chunks], refs[2 * chunks : 2 * chunks + parts]
+def project_body(count, chunks, has_acc, index_ref, *refs):
+    mine, theirs, weights = refs[:chunks], refs[chunks : 2 * chunks], refs[2 * chunks : (2 + count) * chunks]
     out_ref = refs[-1]
     tile = mine[0].shape[0]
     rows = jnp.concatenate(
         [jnp.concatenate([ref[...] for ref in mine], axis=1), jnp.concatenate([ref[...] for ref in theirs], axis=1)], axis=0
     )
     for c in range(count):
-        cuts = [ref.shape[0] // count for ref in weights]
-        w = jnp.concatenate([ref[c * cut : (c + 1) * cut, :] for ref, cut in zip(weights, cuts)], axis=0)
+        w = jnp.concatenate([ref[...] for ref in weights[c * chunks : (c + 1) * chunks]], axis=0)
         total = jnp.dot(rows, w, preferred_element_type=F32)
         for place in range(2):
             part = total[place * tile : (place + 1) * tile]
@@ -64,14 +41,19 @@
             out_ref[place, c] = part.astype(out_ref.dtype)
 
 
-def project(count, depth, index, mine, theirs, weights, acc, last):
+def project(first, count, index, mine, theirs, weights, acc, last):
     rows, width = mine.shape[0], weights[0].shape[1]
-    tile, chunks, parts = rows // 4, len(index), len(weights)
+    depth = weights[0].shape[0] // 3
+    tile, chunks = rows // 4, len(index)
     token_specs = [pl.BlockSpec((tile, depth), functools.partial(lambda n, i, ref: (i, ref[n]), n)) for n in range(chunks)]
-    weight_specs = [pl.BlockSpec(part.shape, lambda i, ref: (0, 0)) for part in weights]
+    weight_specs = [
+        pl.BlockSpec((depth, width), functools.partial(lambda c, i, ref: (c, 0), first + c))
+        for c in range(count)
+        for _ in range(chunks)
+    ]
     acc_spec = pl.BlockSpec((2, count, tile, width), lambda i, ref: (0, 0, i, 0))
     return pl.pallas_call(
-        functools.partial(project_body, count, chunks, parts, acc is not None),
+        functools.partial(project_body, count, chunks, acc is not None),
         out_shape=jax.ShapeDtypeStruct((2, count, rows, width), BF16 if last else F32),
         grid_spec=pltpu.PrefetchScalarGridSpec(
             num_scalar_prefetch=1,
@@ -83,7 +65,13 @@
         cost_estimate=pl.CostEstimate(
             flops=4 * rows * depth * chunks * count * width, bytes_accessed=4 * rows * depth * chunks, transcendentals=0
         ),
-    )(jnp.stack(index), *([mine] * chunks), *([theirs] * chunks), *weights, *([] if acc is None else [acc]))
+    )(
+        jnp.stack(index),
+        *([mine] * chunks),
+        *([theirs] * chunks),
+        *(list(weights) * count),
+        *([] if acc is None else [acc]),
+    )
 
 
 def join(earlier, later):
@@ -172,56 +160,52 @@
     )(scalar, *args)
 
 
-def attend_body(scale, q_ref, kv_ref, column_ref, row_ref, state_ref, out_ref, square_ref):
+def intra_body(scale, q_ref, kv_ref, column_ref, row_ref, out_ref):
     rows, width = q_ref.shape[2:]
-    across = (((1,), (1,)), ((), ()))
     i, j = (lax.broadcasted_iota(jnp.int32, (DH, DH), axis) for axis in range(2))
-    ones = jnp.ones((8, DH), BF16)
     for start in range(0, rows, DH):
         stop = start + DH
-        squares = jnp.zeros((8, DH), F32)
         for h in range(width // DH):
             cut = slice(h * DH, (h + 1) * DH)
             q = q_ref[0, 0, start:stop, cut]
             column, row = column_ref[0, h, start:stop], row_ref[0, h, :, :stop]
-            raw = lax.dot_general(q, kv_ref[0, 0, :stop, cut], across, preferred_element_type=F32) * scale
+            raw = lax.dot_general(q, kv_ref[0, 0, :stop, cut], ACROSS, preferred_element_type=F32) * scale
             gap = jnp.where(i >= j, column - row[:, start:], -1e30)
             scores = (raw[:, start:] * jnp.exp(gap)).astype(BF16)
             if start:
                 border = row[:, start - 1 : start]
                 faded = raw[:, :start] * jnp.exp(column - border) * jnp.exp(border - row[:, :start])
                 scores = jnp.concatenate([faded.astype(BF16), scores], axis=1)
-            intra = jnp.dot(scores, kv_ref[0, 1, :stop, cut], preferred_element_type=F32)
-            inter = jnp.dot(jnp.concatenate([q] * 3, axis=1), state_ref[0, h], preferred_element_type=F32)
-            attended = intra + inter * (jnp.exp(column) * scale)
-            out_ref[0, start:stop, cut] = attended
-            for part in split(attended * attended, 2):
-                squares += lax.dot_general(ones, part.astype(BF16), across, preferred_element_type=F32)
-        square_ref[0, :, start:stop] = squares
-
-
-def attend(q, kv, column, row, state):
-    _, _, rows, width = q.shape
-    group = width // DH
-
+            out_ref[0, start:stop, cut] = jnp.dot(scores, kv_ref[0, 1, :stop, cut], preferred_element_type=F32)
+
+
+def inter_body(scale, q_ref, column_ref, intra_ref, state_ref, out_ref, square_ref):
+    rows, width = q_ref.shape[2:]
+    squares = jnp.zeros((8, rows), F32)
+    for h in range(width // DH):
+        cut = slice(h * DH, (h + 1) * DH)
+        q = q_ref[0, 0, :, cut]
+        inter = jnp.dot(jnp.concatenate([q] * 3, axis=1), state_ref[0, h], preferred_element_type=F32)
+        attended = intra_ref[0, :, cut] + inter * (jnp.exp(column_ref[0, h]) * scale)
+        out_ref[0, :, cut] = attended
+        for part in split(attended * attended, 2):
+            squares += lax.dot_general(jnp.ones((8, DH), BF16), part.astype(BF16), ACROSS, preferred_element_type=F32)
+    square_ref[0] = squares
+
+
+def by_place(body, outs, flops, *args):
     def whole(shape):
-        return pl.BlockSpec((1,) + shape, lambda a: (a,) + (0,) * len(shape))
+        return pl.BlockSpec((1,) + shape[1:], lambda a: (a,) + (0,) * (len(shape) - 1))
 
     return pl.pallas_call(
-        functools.partial(attend_body, DH**-0.5),
-        out_shape=[jax.ShapeDtypeStruct((2, rows, width), F32), jax.ShapeDtypeStruct((2, 8, rows), F32)],
+        functools.partial(body, DH**-0.5),
+        out_shape=[jax.ShapeDtypeStruct(shape, F32) for shape in outs],
         grid=(2,),
-        in_specs=[
-            whole((1, rows, width)),
-            whole((2, rows, width)),
-            whole((group, rows, 1)),
-            whole((group, 1, rows)),
-            whole((group, 3 * DH, DH)),
-        ],
-        out_specs=[whole((rows, width)), whole((8, rows))],
+        in_specs=[whole(arg.shape) for arg in args],
+        out_specs=[whole(shape) for shape in outs],
         compiler_params=pltpu.CompilerParams(vmem_limit_bytes=VMEM_LIMIT),
-        cost_estimate=pl.CostEstimate(flops=4 * 10**9, bytes_accessed=6 * 10**6, transcendentals=10**6),
-    )(q, kv, column, row, state)
+        cost_estimate=pl.CostEstimate(flops=flops, bytes_accessed=4 * 10**6, transcendentals=10**6),
+    )(*args)
 
 
 def on_device(tokens, w_qkv, log_decay, gain):
@@ -250,28 +234,58 @@
 
     columns = [x, (x + 3) % 4, (x + 1) % 4, (x + 2) % 4]
     index = [[(4 * c + (z + 4 - d) % 4).astype(jnp.int32) for d in range(4)] for c in columns]
-
-    depth = own.shape[1]
-    slots = gather_kv(own[1:].reshape(2 * depth, width))
-    q_early, q_late = gather_q(own[0])
-    early = [(d, n) for d in (0, 1) for n in (0, 1, 2)] + [(0, 3)]
-    late = [(d, n) for d in range(4) for n in range(4) if (d, n) not in early]
-    kv = None
-    for some in (early, late):
-        chunk = [index[n][d] for d, n in some]
-        kv = project(2, depth, chunk, tokens, other_tokens, [slots[d][n] for d, n in some], kv, some is late)
-
+    own_x, right_x, left_x, far_x = index
+
+    def along_z(part):
+        return lax.ppermute(part, "zl", NEXT)
+
+    def to_right(part):
+        return lax.ppermute(part, "x", NEXT)
+
+    def to_left(part):
+        return lax.ppermute(part, "x", LAST)
+
+    def partial(parts, chunks, acc):
+        kv = project(1, 2, chunks, tokens, other_tokens, parts, acc and acc[0], False)
+        return kv, project(0, 1, chunks, tokens, other_tokens, parts, acc and acc[1], False)
+
+    step = lax.optimization_barrier
+    own = own.reshape(-1, width)
+    half = own.shape[0] // 2
+    a1, r0, l0 = along_z(own), to_right(own), to_left(own)
+    a1, r0, l0, other_tokens, cumulative, column, totals = step((a1, r0, l0, other_tokens, cumulative, column, totals))
+
+    a2, r1, l1, f0, g0 = along_z(a1), to_right(a1), to_left(a1), to_right(r0[:half]), to_left(l0[half:])
+    acc = partial([own, a1, r0, l0], [own_x[0], own_x[1], right_x[0], left_x[0]], None)
+    a2, r1, l1, f0, g0, acc = step((a2, r1, l1, f0, g0, acc))
+
+    far0 = jnp.concatenate([f0, g0])
+    a3, r2, l2 = along_z(a2), to_right(a2), to_left(a2)
+    acc = partial([a2, r1, l1, far0], [own_x[2], right_x[1], left_x[1], far_x[0]], acc)
+    a3, r2, l2, acc, far0 = step((a3, r2, l2, acc, far0))
+
+    b1, r3, l3 = along_z(far0), to_right(a3), to_left(a3)
+    acc = partial([a3, r2, l2], [own_x[3], right_x[2], left_x[2]], acc)
+    b1, r3, l3, acc = step((b1, r3, l3, acc))
+
+    b2, f3, g3 = along_z(b1), to_right(r3[:half]), to_left(l3[half:])
+    acc = partial([b1, r3, l3], [far_x[1], right_x[3], left_x[3]], acc)
+    b2, f3, g3, acc = step((b2, f3, g3, acc))
+
+    last = [b2, jnp.concatenate([f3, g3])], [far_x[2], far_x[3]]
+    kv = project(1, 2, last[1], tokens, other_tokens, last[0], acc[0], True)
     shape = (group, DH + TAIL, DH)
     chip, sent, first = small_kernel(state_body, [(shape, F32), (shape, BF16), (shape, F32)], place, kv, column, totals)
     backs = [lax.ppermute(sent, "zl", [(i, (i + j) % 4) for i in range(4)]) for j in (1, 2, 3)]
+    q = project(0, 1, last[1], tokens, other_tokens, last[0], tied(acc[1], sent), True)
     before, row = small_kernel(row_body, [(shape, F32), (shape, BF16)], z.reshape(1), chip, *backs)
+    row, q = step((row, q))
     backs = [lax.ppermute(row, "x", [(i, i + j) for i in range(4 - j)]) for j in (1, 2, 3)]
+    (intra,) = by_place(intra_body, [(2, rows, width)], 4 * 10**9, q, kv, column, cumulative[:, :, None, :])
+    backs, intra = step((backs, intra))
     (state,) = small_kernel(incoming_body, [((2, group, 3 * DH, DH), BF16)], place, before, first, *backs)
 
-    q = project(1, depth, sum(index[:3], []), tokens, other_tokens, q_early, None, False)
-    q = project(1, depth, index[3], tokens, other_tokens, q_late, q, True)
-
-    attended, squares = attend(q, kv, column, cumulative[:, :, None, :], state)
+    attended, squares = by_place(inter_body, [(2, rows, width), (2, 8, rows)], 10**9, q, column, intra, state)
     squares = squares[:, 0, :]
     summed = squares[0] + lax.ppermute(squares[1], "core", SWAP)
     got = lax.ppermute(attended[1], "core", SWAP)

time: 194 us -> 154 us (0.79)
  waiting for transfers between devices: 76.7 us -> 24.8 us
  Pallas kernels: 37.4 us -> 56.2 us
  starting transfers between devices: 53.7 us -> 46.9 us
  other arithmetic: 9.2 us -> 3.28 us
  local copies, waits for them, and re-layouts: 15.6 us -> 21.3 us
    ppermute x24 -> x17, waiting for transfers between devices: 66.4 us -> 6.96 us  [the longest x5 3.68 us: along_z(): return lax.ppermute(part, 'zl', NEXT)]
    pallas_call x5 -> x12, Pallas kernels: 36.3 us -> 55 us  [the longest x10 49.4 us: project(): pl.pallas_call(functools.partial(project_body, count, chunks, acc is not...]
    unnamed x27 -> x38, local copies, waits for them, and re-layouts: 4 us -> 14.2 us
    ppermute x1, waiting for transfers between devices: 0.01 us -> 6.98 us  [on_device(): decay = jnp.stack([kept, lax.ppermute(tied(sent, own), 'core', SWAP)])]
    slice x8 -> x5, local copies, waits for them, and re-layouts: 5.89 us -> 1.65 us  [the longest x1 0.73 us: on_device(): r0[:half]]
    another operation x3, other arithmetic: 5.41 us -> 1.57 us
    ppermute x24 -> x17, starting transfers between devices: 29.4 us -> 26 us  [the longest x6 14.1 us: to_left(): return lax.ppermute(part, 'x', LAST)]
    optimization_barrier x0 -> x1, local copies, waits for them, and re-layouts: none -> 2.27 us  [on_device(): step((a1, r0, l0, other_tokens, cumulative, column, totals))]
  transfers between devices with their start and end apart: 39 -> 32, of which waited for: 14 -> 10; matrix products, arithmetic and copies ran while one was open for 10% -> 6% of each run, Pallas kernels for 16% -> 32%
where the time goes in v1:
time: 154 us; the launch traced here: 153 us
  Pallas kernels  56.2 us (36%)
  starting transfers between devices  46.9 us (30%)
  waiting for transfers between devices  24.8 us (16%)
  local copies, waits for them, and re-layouts  21.3 us (14%)
  other arithmetic  3.28 us (2%)
    pallas_call x10, Pallas kernels, project(): pl.pallas_call(functools.partial(project_body, count, chunks, acc is not...  49.4 us
    unnamed x38, local copies, waits for them, and re-layouts  14.2 us
    ppermute x6, starting transfers between devices, to_left(): return lax.ppermute(part, 'x', LAST)  14.1 us
    ppermute x5, starting transfers between devices, along_z(): return lax.ppermute(part, 'zl', NEXT)  7.63 us
    ppermute x1, waiting for transfers between devices, on_device(): decay = jnp.stack([kept, lax.ppermute(tied(sent, own), 'core', SWAP)])  6.98 us
    ppermute x3, starting transfers between devices, on_device(): lax.ppermute(row, 'x', [(i, i + j) for i in range(4 - j)])  6.82 us
    ppermute x3, starting transfers between devices, on_device(): lax.ppermute(sent, 'zl', [(i, (i + j) % 4) for i in range(4)])  5.65 us
    pallas_call x2, Pallas kernels, by_place(): pl.pallas_call(functools.partial(body, DH ** (-0.5)), out_shape=[jax.Shap...  5.59 us
  transfers between devices with their start and end apart: 32, of which 10 were waited for; matrix products, arithmetic and copies ran while one was open for 6% of the time, Pallas kernels for 32%

profile of v1, /device:TPU:24, one launch (start us, length us, event | category | flops | bytes accessed | tf_op | source)
XLA Modules:
  0.0 152.8 jit_solution(8984144313060307440)
XLA Ops:
  0.0 1.1 constant_dynamic-slice_fusion.3
  1.2 1.6 %collective-permute-done = bf16[3,192,256]{2,1,0:T(8,128)(2,1)S(1)} collective-permute-done((bf16[3,192,256]{2,1,0:T(8,128)(2,1)S(1)}, bf16[3,192,256]{2,1,0:T(8,128)(2,1)S(1)}, u32[]{:S(2)}, u32[]{:S(2)}) %collective-permute-start) | collective-permute-done | bytes 294944 | tf_op jit(solution)/shard_map/ppermute | solution.py:225
  3.3 1.9 %collective-permute-start.1 = (bf16[1152,256]{1,0:T(8,128)(2,1)S(1)}, bf16[1152,256]{1,0:T(8,128)(2,1)S(1)}, u32[]{:S(2)}, u32[]{:S(2)}) collective-permute-start(bf16[1152,256]{1,0:T(8,128)(2,1)S(1)} %bitcast.24), channel_id=1, source_target_pairs={{0,16},{16,32},{32,48},{48,0},{1,17},{17,33},{33,49},{49,1},{2,18}... | collective-permute-start | bytes 1769480 | tf_op jit(solution)/shard_map/ppermute | solution.py:240
  5.2 1.5 collective-permute-start.2
  6.7 1.7 %collective-permute-start.3 = (bf16[1152,256]{1,0:T(8,128)(2,1)S(1)}, bf16[1152,256]{1,0:T(8,128)(2,1)S(1)}, u32[]{:S(2)}, u32[]{:S(2)}) collective-permute-start(bf16[1152,256]{1,0:T(8,128)(2,1)S(1)} %bitcast.26), channel_id=1, source_target_pairs={{0,192},{64,0},{128,64},{192,128},{1,193},{65,1},{129,65},{193,129... | collective-permute-start | bytes 1769480 | tf_op jit(solution)/shard_map/ppermute | solution.py:246
  8.6 7.0 %collective-permute-done.5 = f32[2,640]{1,0:T(2,128)S(1)} collective-permute-done((f32[2,640]{1,0:T(2,128)S(1)}, f32[2,640]{1,0:T(2,128)S(1)}, u32[]{:S(2)}, u32[]{:S(2)}) %collective-permute-start.5) | collective-permute-done | bytes 5152 | tf_op jit(solution)/shard_map/ppermute | solution.py:228
  15.6 1.1 reduce-window.6
  17.3 0.6 reduce_window_sum.27
  18.1 3.7 %collective-permute-done.1.refs_9_.refs_13_ = bf16[1152,256]{1,0:T(8,128)(2,1)S(1)} collective-permute-done((bf16[1152,256]{1,0:T(8,128)(2,1)S(1)}, bf16[1152,256]{1,0:T(8,128)(2,1)S(1)}, u32[]{:S(2)}, u32[]{:S(2)}) %collective-permute-start.1) | collective-permute-done | bytes 589856 | tf_op jit(solution)/shard_map/ppermute | solution.py:240
  21.8 1.9 %collective-permute-start.6 = (bf16[1152,256]{1,0:T(8,128)(2,1)S(1)}, bf16[1152,256]{1,0:T(8,128)(2,1)S(1)}, u32[]{:S(2)}, u32[]{:S(2)}) collective-permute-start(bf16[1152,256]{1,0:T(8,128)(2,1)S(1)} %collective-permute-done.1.refs_9_.refs_13_), channel_id=1, source_target_pairs={{0,16},{16,32},{32,48},{48,0},{1,17},{17,33},{33,49},{49,1},{2,18}... | collective-permute-start | bytes 1769480 | tf_op jit(solution)/shard_map/ppermute | solution.py:240
  23.7 1.5 collective-permute-start.7
  25.2 1.8 %collective-permute-start.8 = (bf16[1152,256]{1,0:T(8,128)(2,1)S(1)}, bf16[1152,256]{1,0:T(8,128)(2,1)}, u32[]{:S(2)}, u32[]{:S(2)}) collective-permute-start(bf16[1152,256]{1,0:T(8,128)(2,1)S(1)} %collective-permute-done.1.refs_9_.refs_13_), channel_id=1, source_target_pairs={{0,192},{64,0},{128,64},{192,128},{1,193},{65,1},{129,65},{193,129... | collective-permute-start | bytes 1769480 | tf_op jit(solution)/shard_map/ppermute | solution.py:246
  27.0 0.7 slice.42
  27.7 1.7 %collective-permute-start.10 = (bf16[576,256]{1,0:T(8,128)(2,1)}, bf16[576,256]{1,0:T(8,128)(2,1)}, u32[]{:S(2)}, u32[]{:S(2)}) collective-permute-start(bf16[576,256]{1,0:T(8,128)(2,1)} %slice.42), channel_id=1, source_target_pairs={{0,192},{64,0},{128,64},{192,128},{1,193},{65,1},{129,65},{193,129... | collective-permute-start | bytes 884744 | tf_op jit(solution)/shard_map/ppermute | solution.py:246
  29.4 0.7 slice.41
  30.5 4.7 %shard_map.47.refs_12_ = f32[2,1,640,256]{3,2,1,0:T(8,128)S(1)} custom-call(s32[4]{0:T(128)S(1)} %pad_add_fusion.1.index_ref, bf16[640,6144]{1,0:T(8,128)(2,1)} %refs_1_.19, bf16[640,6144]{1,0:T(8,128)(2,1)} %refs_1_.19, bf16[640,6144]{1,0:T(8,128)(2,1)} %refs_1_.19, bf16[640,6144]{1,0:T(8,128)(2,1)} %refs_1_.19, ...), custom_call_target="tpu_custom_call" | custom-call | flops 1006632960 | bytes 3932160 | tf_op jit(solution)/shard_map/pallas_call | solution.py:55
  35.2 5.5 %shard_map.46.refs_16_ = f32[2,2,640,256]{3,2,1,0:T(8,128)S(1)} custom-call(s32[4]{0:T(128)S(1)} %pad_add_fusion.1.index_ref, bf16[640,6144]{1,0:T(8,128)(2,1)} %refs_1_.19, bf16[640,6144]{1,0:T(8,128)(2,1)} %refs_1_.19, bf16[640,6144]{1,0:T(8,128)(2,1)} %refs_1_.19, bf16[640,6144]{1,0:T(8,128)(2,1)} %refs_1_.19, ...), custom_call_target="tpu_custom_call" | custom-call | flops 2013265920 | bytes 3932160 | tf_op jit(solution)/shard_map/pallas_call | solution.py:55
  40.7 1.6 %copy-done.2 = f32[2,2,640,256]{3,2,1,0:T(8,128)} copy-done((f32[2,2,640,256]{3,2,1,0:T(8,128)}, f32[2,2,640,256]{3,2,1,0:T(8,128)S(1)}, u32[]{:S(2)}) %copy-start.2) | copy-done | bytes 2621464
  42.3 2.9 %collective-permute-done.10 = bf16[576,256]{1,0:T(8,128)(2,1)} collective-permute-done((bf16[576,256]{1,0:T(8,128)(2,1)}, bf16[576,256]{1,0:T(8,128)(2,1)}, u32[]{:S(2)}, u32[]{:S(2)}) %collective-permute-start.10) | collective-permute-done | bytes 294944 | tf_op jit(solution)/shard_map/ppermute | solution.py:246
  45.6 2.0 %collective-permute-start.11 = (bf16[1152,256]{1,0:T(8,128)(2,1)S(1)}, bf16[1152,256]{1,0:T(8,128)(2,1)}, u32[]{:S(2)}, u32[]{:S(2)}) collective-permute-start(bf16[1152,256]{1,0:T(8,128)(2,1)S(1)} %collective-permute-done.6.refs_8_.refs_12_), channel_id=1, source_target_pairs={{0,16},{16,32},{32,48},{48,0},{1,17},{17,33},{33,49},{49,1},{2,18}... | collective-permute-start | bytes 1769480 | tf_op jit(solution)/shard_map/ppermute | solution.py:240
  47.6 0.9 collective-permute-start.12
  48.5 2.4 %collective-permute-start.13 = (bf16[1152,256]{1,0:T(8,128)(2,1)S(1)}, bf16[1152,256]{1,0:T(8,128)(2,1)S(1)}, u32[]{:S(2)}, u32[]{:S(2)}) collective-permute-start(bf16[1152,256]{1,0:T(8,128)(2,1)S(1)} %collective-permute-done.6.refs_8_.refs_12_), channel_id=1, source_target_pairs={{0,192},{64,0},{128,64},{192,128},{1,193},{65,1},{129,65},{193,129... | collective-permute-start | bytes 1769480 | tf_op jit(solution)/shard_map/ppermute | solution.py:246
  50.9 1.0 constant_dynamic-update-slice_fusion.1
  51.9 1.0 constant_dynamic-update-slice_fusion.refs_11_.refs_15_
  52.9 4.8 %shard_map.49.refs_9_ = f32[2,1,640,256]{3,2,1,0:T(8,128)S(1)} custom-call(s32[4]{0:T(128)S(1)} %pad_add_fusion.2.index_ref, bf16[640,6144]{1,0:T(8,128)(2,1)} %refs_1_.19, bf16[640,6144]{1,0:T(8,128)(2,1)} %refs_1_.19, bf16[640,6144]{1,0:T(8,128)(2,1)} %refs_1_.19, bf16[640,6144]{1,0:T(8,128)(2,1)} %refs_1_.19, ...), custom_call_target="tpu_custom_call" | custom-call | flops 1006632960 | bytes 3932160 | tf_op jit(solution)/shard_map/pallas_call | solution.py:55
  57.7 1.0 copy-done.10
  58.8 6.2 %shard_map.48.refs_12_ = f32[2,2,640,256]{3,2,1,0:T(8,128)S(1)} custom-call(s32[4]{0:T(128)S(1)} %pad_add_fusion.2.index_ref, bf16[640,6144]{1,0:T(8,128)(2,1)} %refs_1_.19, bf16[640,6144]{1,0:T(8,128)(2,1)} %refs_1_.19, bf16[640,6144]{1,0:T(8,128)(2,1)} %refs_1_.19, bf16[640,6144]{1,0:T(8,128)(2,1)} %refs_1_.19, ...), custom_call_target="tpu_custom_call" | custom-call | flops 2013265920 | bytes 3932160 | tf_op jit(solution)/shard_map/pallas_call | solution.py:55
  65.0 1.6 %copy-done = f32[2,2,640,256]{3,2,1,0:T(8,128)} copy-done((f32[2,2,640,256]{3,2,1,0:T(8,128)}, f32[2,2,640,256]{3,2,1,0:T(8,128)S(1)}, u32[]{:S(2)}) %copy-start) | copy-done | bytes 2621464
  66.5 0.8 copy-done.3
  67.3 0.8 copy-done.6
  68.7 3.2 %collective-permute-start.16 = (bf16[1152,256]{1,0:T(8,128)(2,1)}, bf16[1152,256]{1,0:T(8,128)(2,1)S(1)}, u32[]{:S(2)}, u32[]{:S(2)}) collective-permute-start(bf16[1152,256]{1,0:T(8,128)(2,1)} %collective-permute-done.11.refs_6_.refs_9_), channel_id=1, source_target_pairs={{0,192},{64,0},{128,64},{192,128},{1,193},{65,1},{129,65},{193,129... | collective-permute-start | bytes 1769480 | tf_op jit(solution)/shard_map/ppermute | solution.py:246
  72.1 1.1 copy-done.4
  73.1 1.1 copy-done.7
  74.2 1.3 copy-done.11
  75.5 4.5 %shard_map.51.refs_9_ = f32[2,1,640,256]{3,2,1,0:T(8,128)S(1)} custom-call(s32[3]{0:T(128)S(1)} %pad_add_fusion.3.index_ref, bf16[640,6144]{1,0:T(8,128)(2,1)} %refs_1_.19, bf16[640,6144]{1,0:T(8,128)(2,1)} %refs_1_.19, bf16[640,6144]{1,0:T(8,128)(2,1)} %refs_1_.19, bf16[640,6144]{1,0:T(8,128)(2,1)} %collective-permute-done.4.refs_4_.refs_5_.refs_6_.refs_7_.refs_3_.refs_2_, ...), custom_call_target="tpu_custom_call" | custom-call | flops 754974720 | bytes 2949120 | tf_op jit(solution)/shard_map/pallas_call | solution.py:55
  80.0 1.0 copy-done.12
  81.0 5.7 %shard_map.50.refs_12_ = f32[2,2,640,256]{3,2,1,0:T(8,128)S(1)} custom-call(s32[3]{0:T(128)S(1)} %pad_add_fusion.3.index_ref, bf16[640,6144]{1,0:T(8,128)(2,1)} %refs_1_.19, bf16[640,6144]{1,0:T(8,128)(2,1)} %refs_1_.19, bf16[640,6144]{1,0:T(8,128)(2,1)} %refs_1_.19, bf16[640,6144]{1,0:T(8,128)(2,1)} %collective-permute-done.4.refs_4_.refs_5_.refs_6_.refs_7_.refs_3_.refs_2_, ...), custom_call_target="tpu_custom_call" | custom-call | flops 1509949440 | bytes 2949120 | tf_op jit(solution)/shard_map/pallas_call | solution.py:55
  86.7 1.6 %copy-done.1 = f32[2,2,640,256]{3,2,1,0:T(8,128)} copy-done((f32[2,2,640,256]{3,2,1,0:T(8,128)}, f32[2,2,640,256]{3,2,1,0:T(8,128)S(1)}, u32[]{:S(2)}) %copy-start.1) | copy-done | bytes 2621464
  88.3 1.3 collective-permute-start.17
  89.8 3.3 %collective-permute-start.19 = (bf16[576,256]{1,0:T(8,128)(2,1)S(1)}, bf16[576,256]{1,0:T(8,128)(2,1)S(1)}, u32[]{:S(2)}, u32[]{:S(2)}) collective-permute-start(bf16[576,256]{1,0:T(8,128)(2,1)S(1)} %slice.44), channel_id=1, source_target_pairs={{0,192},{64,0},{128,64},{192,128},{1,193},{65,1},{129,65},{193,129... | collective-permute-start | bytes 884744 | tf_op jit(solution)/shard_map/ppermute | solution.py:246
  93.1 2.3 %copy.5.column_ref = f32[2,2,640,1]{3,2,1,0:T(8,128)} copy(f32[2,2,640,1]{2,1,0,3:T(2,128)} %reduce_window_sum.27) | data formatting | bytes 20480 | tf_op jit(solution)/shard_map/optimization_barrier | solution.py:256
  95.4 1.3 copy-done.13
  96.7 4.4 %shard_map.53.refs_6_ = f32[2,1,640,256]{3,2,1,0:T(8,128)S(1)} custom-call(s32[3]{0:T(128)S(1)} %pad_add_fusion.4.index_ref, bf16[640,6144]{1,0:T(8,128)(2,1)} %refs_1_.19, bf16[640,6144]{1,0:T(8,128)(2,1)} %refs_1_.19, bf16[640,6144]{1,0:T(8,128)(2,1)} %refs_1_.19, bf16[640,6144]{1,0:T(8,128)(2,1)} %collective-permute-done.4.refs_4_.refs_5_.refs_6_.refs_7_.refs_3_.refs_2_, ...), custom_call_target="tpu_custom_call" | custom-call | flops 754974720 | bytes 2949120 | tf_op jit(solution)/shard_map/pallas_call | solution.py:55
  101.1 5.6 %shard_map.52.refs_8_ = f32[2,2,640,256]{3,2,1,0:T(8,128)S(1)} custom-call(s32[3]{0:T(128)S(1)} %pad_add_fusion.4.index_ref, bf16[640,6144]{1,0:T(8,128)(2,1)} %refs_1_.19, bf16[640,6144]{1,0:T(8,128)(2,1)} %refs_1_.19, bf16[640,6144]{1,0:T(8,128)(2,1)} %refs_1_.19, bf16[640,6144]{1,0:T(8,128)(2,1)} %collective-permute-done.4.refs_4_.refs_5_.refs_6_.refs_7_.refs_3_.refs_2_, ...), custom_call_target="tpu_custom_call" | custom-call | flops 1509949440 | bytes 2949120 | tf_op jit(solution)/shard_map/pallas_call | solution.py:55
  106.8 4.3 %shard_map.54.kv_ref = bf16[2,2,640,256]{3,2,1,0:T(8,128)(2,1)S(1)} custom-call(s32[2]{0:T(128)S(1)} %pad_add_fusion.index_ref, bf16[640,6144]{1,0:T(8,128)(2,1)} %refs_1_.19, bf16[640,6144]{1,0:T(8,128)(2,1)} %refs_1_.19, bf16[640,6144]{1,0:T(8,128)(2,1)} %collective-permute-done.4.refs_4_.refs_5_.refs_6_.refs_7_.refs_3_.refs_2_, ...), custom_call_target="tpu_custom_call" | custom-call | flops 1006632960 | bytes 1966080 | tf_op jit(solution)/shard_map/pallas_call | solution.py:55
  111.1 0.9 shard_map.55
  112.0 1.4 collective-permute-start.20
  113.3 1.9 %collective-permute-start.21 = (bf16[2,144,128]{2,1,0:T(8,128)(2,1)S(1)}, bf16[2,144,128]{2,1,0:T(8,128)(2,1)S(1)}, u32[]{:S(2)}, u32[]{:S(2)}) collective-permute-start(bf16[2,144,128]{2,1,0:T(8,128)(2,1)S(1)} %get-tuple-element.82), channel_id=1, source_target_pairs={{0,32},{16,48},{32,0},{48,16},{1,33},{17,49},{33,1},{49,17},{2,34}... | collective-permute-start | bytes 221192 | tf_op jit(solution)/shard_map/ppermute | solution.py:279
  115.2 2.4 %collective-permute-start.22 = (bf16[2,144,128]{2,1,0:T(8,128)(2,1)S(1)}, bf16[2,144,128]{2,1,0:T(8,128)(2,1)S(1)}, u32[]{:S(2)}, u32[]{:S(2)}) collective-permute-start(bf16[2,144,128]{2,1,0:T(8,128)(2,1)S(1)} %get-tuple-element.82), channel_id=1, source_target_pairs={{0,48},{16,0},{32,16},{48,32},{1,49},{17,1},{33,17},{49,33},{2,50}... | collective-permute-start | bytes 221192 | tf_op jit(solution)/shard_map/ppermute | solution.py:279
  117.6 3.8 %shard_map.57.q_ref = bf16[2,1,640,256]{3,2,1,0:T(8,128)(2,1)S(1)} custom-call(s32[2]{0:T(128)S(1)} %pad_add_fusion.index_ref, bf16[640,6144]{1,0:T(8,128)(2,1)} %refs_1_.19, bf16[640,6144]{1,0:T(8,128)(2,1)} %refs_1_.19, bf16[640,6144]{1,0:T(8,128)(2,1)} %collective-permute-done.4.refs_4_.refs_5_.refs_6_.refs_7_.refs_3_.refs_2_, ...), custom_call_target="tpu_custom_call" | custom-call | flops 503316480 | bytes 1966080 | tf_op jit(solution)/shard_map/pallas_call | solution.py:55
  121.7 1.3 collective-permute-start.23
  123.0 4.0 %collective-permute-start.24 = (bf16[2,144,128]{2,1,0:T(8,128)(2,1)S(1)}, bf16[2,144,128]{2,1,0:T(8,128)(2,1)S(1)}, u32[]{:S(2)}, u32[]{:S(2)}) collective-permute-start(bf16[2,144,128]{2,1,0:T(8,128)(2,1)S(1)} %get-tuple-element.87), channel_id=1, source_target_pairs={{0,128},{64,192},{1,129},{65,193},{2,130},{66,194},{3,131},{67,195... | collective-permute-start | bytes 221192 | tf_op jit(solution)/shard_map/ppermute | solution.py:283
  127.0 1.5 collective-permute-start.25
  128.5 3.5 %shard_map.58.intra_ref = f32[2,640,256]{2,1,0:T(8,128)S(1)} custom-call(bf16[2,1,640,256]{3,2,1,0:T(8,128)(2,1)S(1)} %shard_map.57.q_ref, bf16[2,2,640,256]{3,2,1,0:T(8,128)(2,1)S(1)} %shard_map.54.kv_ref, f32[2,2,640,1]{3,2,1,0:T(8,128)S(1)} %copy-done.9, f32[2,2,1,640]{3,2,1,0:T(1,128)S(1)} %broadcast_in_dim.15.row_ref), custom_call_target="tpu_custom_call" | custom-call | flops 4000000000 | bytes 4000000 | tf_op jit(solution)/shard_map/pallas_call | solution.py:200
  132.2 2.1 %shard_map.60 = (f32[2,640,256]{2,1,0:T(8,128)S(1)}, f32[2,8,640]{2,1,0:T(8,128)S(1)}) custom-call(bf16[2,1,640,256]{3,2,1,0:T(8,128)(2,1)S(1)} %shard_map.57.q_ref, f32[2,2,640,1]{3,2,1,0:T(8,128)S(1)} %copy-done.9, f32[2,640,256]{2,1,0:T(8,128)S(1)} %shard_map.58.intra_ref, bf16[2,2,384,128]{3,2,1,0:T(8,128)(2,1)S(1)} %shard_map.59.state_ref), custom_call_target="tpu_custom_call" | custom-call | flops 1000000000 | bytes 4000000 | tf_op jit(solution)/shard_map/pallas_call | solution.py:200
  134.5 0.6 collective-permute-start.27
  135.1 1.5 collective-permute-done.27
  136.8 2.6 %collective-permute-start.29 = (f32[640]{0:T(1024)S(1)}, f32[640]{0:T(1024)S(1)}, u32[]{:S(2)}, u32[]{:S(2)}) collective-permute-start(f32[640]{0:T(1024)S(1)} %add.182), channel_id=1, source_target_pairs={{0,4},{2,6},{4,0},{6,2},{1,5},{3,7},{5,1},{7,3},{8,12},{10,14},{12... | collective-permute-start | bytes 7688 | tf_op jit(solution)/shard_map/ppermute | solution.py:292
  139.4 0.8 collective-permute-done.28
  140.2 1.7 %collective-permute-done.29 = f32[640]{0:T(1024)S(1)} collective-permute-done((f32[640]{0:T(1024)S(1)}, f32[640]{0:T(1024)S(1)}, u32[]{:S(2)}, u32[]{:S(2)}) %collective-permute-start.29) | collective-permute-done | bytes 2592 | tf_op jit(solution)/shard_map/ppermute | solution.py:292
  141.9 2.3 %collective-permute-done.30 = f32[640]{0:T(1024)S(1)} collective-permute-done((f32[640]{0:T(1024)S(1)}, f32[640]{0:T(1024)S(1)}, u32[]{:S(2)}, u32[]{:S(2)}) %collective-permute-start.30) | collective-permute-done | bytes 2592 | tf_op jit(solution)/shard_map/ppermute | solution.py:292
  144.2 4.5 %collective-permute-start.31 = (f32[640]{0:T(1024)S(1)}, f32[640]{0:T(1024)S(1)}, u32[]{:S(2)}, u32[]{:S(2)}) collective-permute-start(f32[640]{0:T(1024)S(1)} %add_add_fusion), channel_id=1, source_target_pairs={{0,1},{1,0},{2,3},{3,2},{4,5},{5,4},{6,7},{7,6},{8,9},{9,8},{10,11... | collective-permute-start | bytes 7688 | tf_op jit(solution)/shard_map/ppermute | solution.py:293
  148.8 3.0 %collective-permute-done.31 = f32[640]{0:T(1024)S(1)} collective-permute-done((f32[640]{0:T(1024)S(1)}, f32[640]{0:T(1024)S(1)}, u32[]{:S(2)}, u32[]{:S(2)}) %collective-permute-start.31) | collective-permute-done | bytes 2592 | tf_op jit(solution)/shard_map/ppermute | solution.py:293
  151.8 1.0 fusion.2
  (86 shorter events, 4.1 us)
Async XLA Ops:
  0.0 8.4 %copy-start.16 = (f32[4,640]{1,0:T(4,128)S(1)}, f32[4,640]{1,0:T(4,128)}, u32[]{:S(2)}) copy-start(f32[4,640]{1,0:T(4,128)} %param.6) | copy-start | bytes 30724
  1.1 1.7 %collective-permute-start = (bf16[3,192,256]{2,1,0:T(8,128)(2,1)S(1)}, bf16[3,192,256]{2,1,0:T(8,128)(2,1)S(1)}, u32[]{:S(2)}, u32[]{:S(2)}) collective-permute-start(bf16[3,192,256]{2,1,0:T(8,128)(2,1)S(1)} %get-tuple-element.102), channel_id=1, source_target_pairs={{0,8},{8,0},{1,9},{9,1},{2,10},{10,2},{3,11},{11,3},{4,12},{12,4},... | collective-permute-start | bytes 884744 | tf_op jit(solution)/shard_map/ppermute | solution.py:225
  3.0 18.7 %collective-permute-start.4 = (bf16[640,6144]{1,0:T(8,128)(2,1)}, bf16[640,6144]{1,0:T(8,128)(2,1)}, u32[]{:S(2)}, u32[]{:S(2)}) collective-permute-start(bf16[640,6144]{1,0:T(8,128)(2,1)} %refs_1_.19), channel_id=1, source_target_pairs={{0,8},{8,0},{1,9},{9,1},{2,10},{10,2},{3,11},{11,3},{4,12},{12,4},... | collective-permute-start | bytes 23592968 | tf_op jit(solution)/shard_map/ppermute | solution.py:229
  3.3 18.5 %collective-permute-start.1 = (bf16[1152,256]{1,0:T(8,128)(2,1)S(1)}, bf16[1152,256]{1,0:T(8,128)(2,1)S(1)}, u32[]{:S(2)}, u32[]{:S(2)}) collective-permute-start(bf16[1152,256]{1,0:T(8,128)(2,1)S(1)} %bitcast.24), channel_id=1, source_target_pairs={{0,16},{16,32},{32,48},{48,0},{1,17},{17,33},{33,49},{49,1},{2,18}... | collective-permute-start | bytes 1769480 | tf_op jit(solution)/shard_map/ppermute | solution.py:240
  5.2 16.6 %collective-permute-start.2 = (bf16[1152,256]{1,0:T(8,128)(2,1)S(1)}, bf16[1152,256]{1,0:T(8,128)(2,1)S(1)}, u32[]{:S(2)}, u32[]{:S(2)}) collective-permute-start(bf16[1152,256]{1,0:T(8,128)(2,1)S(1)} %bitcast.25), channel_id=1, source_target_pairs={{0,64},{64,128},{128,192},{192,0},{1,65},{65,129},{129,193},{193,1... | collective-permute-start | bytes 1769480 | tf_op jit(solution)/shard_map/ppermute | solution.py:243
  6.7 15.1 %collective-permute-start.3 = (bf16[1152,256]{1,0:T(8,128)(2,1)S(1)}, bf16[1152,256]{1,0:T(8,128)(2,1)S(1)}, u32[]{:S(2)}, u32[]{:S(2)}) collective-permute-start(bf16[1152,256]{1,0:T(8,128)(2,1)S(1)} %bitcast.26), channel_id=1, source_target_pairs={{0,192},{64,0},{128,64},{192,128},{1,193},{65,1},{129,65},{193,129... | collective-permute-start | bytes 1769480 | tf_op jit(solution)/shard_map/ppermute | solution.py:246
  8.4 7.1 %collective-permute-start.5 = (f32[2,640]{1,0:T(2,128)S(1)}, f32[2,640]{1,0:T(2,128)S(1)}, u32[]{:S(2)}, u32[]{:S(2)}) collective-permute-start(f32[2,640]{1,0:T(2,128)S(1)} %get-tuple-element.52), channel_id=1, source_target_pairs={{0,8},{8,0},{1,9},{9,1},{2,10},{10,2},{3,11},{11,3},{4,12},{12,4},... | collective-permute-start | bytes 15368 | tf_op jit(solution)/shard_map/ppermute | solution.py:228
  17.3 4.5 %copy-start.14 = (f32[2,2,640]{2,1,0:T(2,128)}, f32[2,2,640]{2,1,0:T(2,128)S(1)}, u32[]{:S(2)}) copy-start(f32[2,2,640]{2,1,0:T(2,128)S(1)} %reduce_window_sum.26) | copy-start | bytes 30724
  21.8 23.7 %collective-permute-start.6 = (bf16[1152,256]{1,0:T(8,128)(2,1)S(1)}, bf16[1152,256]{1,0:T(8,128)(2,1)S(1)}, u32[]{:S(2)}, u32[]{:S(2)}) collective-permute-start(bf16[1152,256]{1,0:T(8,128)(2,1)S(1)} %collective-permute-done.1.refs_9_.refs_13_), channel_id=1, source_target_pairs={{0,16},{16,32},{32,48},{48,0},{1,17},{17,33},{33,49},{49,1},{2,18}... | collective-permute-start | bytes 1769480 | tf_op jit(solution)/shard_map/ppermute | solution.py:240
  23.7 21.8 %collective-permute-start.7 = (bf16[1152,256]{1,0:T(8,128)(2,1)S(1)}, bf16[1152,256]{1,0:T(8,128)(2,1)S(1)}, u32[]{:S(2)}, u32[]{:S(2)}) collective-permute-start(bf16[1152,256]{1,0:T(8,128)(2,1)S(1)} %collective-permute-done.1.refs_9_.refs_13_), channel_id=1, source_target_pairs={{0,64},{64,128},{128,192},{192,0},{1,65},{65,129},{129,193},{193,1... | collective-permute-start | bytes 1769480 | tf_op jit(solution)/shard_map/ppermute | solution.py:243
  25.2 20.4 %collective-permute-start.8 = (bf16[1152,256]{1,0:T(8,128)(2,1)S(1)}, bf16[1152,256]{1,0:T(8,128)(2,1)}, u32[]{:S(2)}, u32[]{:S(2)}) collective-permute-start(bf16[1152,256]{1,0:T(8,128)(2,1)S(1)} %collective-permute-done.1.refs_9_.refs_13_), channel_id=1, source_target_pairs={{0,192},{64,0},{128,64},{192,128},{1,193},{65,1},{129,65},{193,129... | collective-permute-start | bytes 1769480 | tf_op jit(solution)/shard_map/ppermute | solution.py:246
  27.7 17.5 %collective-permute-start.10 = (bf16[576,256]{1,0:T(8,128)(2,1)}, bf16[576,256]{1,0:T(8,128)(2,1)}, u32[]{:S(2)}, u32[]{:S(2)}) collective-permute-start(bf16[576,256]{1,0:T(8,128)(2,1)} %slice.42), channel_id=1, source_target_pairs={{0,192},{64,0},{128,64},{192,128},{1,193},{65,1},{129,65},{193,129... | collective-permute-start | bytes 884744 | tf_op jit(solution)/shard_map/ppermute | solution.py:246
  30.2 15.4 %collective-permute-start.9 = (bf16[576,256]{1,0:T(8,128)(2,1)}, bf16[576,256]{1,0:T(8,128)(2,1)}, u32[]{:S(2)}, u32[]{:S(2)}) collective-permute-start(bf16[576,256]{1,0:T(8,128)(2,1)} %slice.41), channel_id=1, source_target_pairs={{0,64},{64,128},{128,192},{192,0},{1,65},{65,129},{129,193},{193,1... | collective-permute-start | bytes 884744 | tf_op jit(solution)/shard_map/ppermute | solution.py:243
  40.7 1.6 %copy-start.2 = (f32[2,2,640,256]{3,2,1,0:T(8,128)}, f32[2,2,640,256]{3,2,1,0:T(8,128)S(1)}, u32[]{:S(2)}) copy-start(f32[2,2,640,256]{3,2,1,0:T(8,128)S(1)} %shard_map.46.refs_16_) | copy-start | bytes 7864324
  45.6 20.9 %collective-permute-start.11 = (bf16[1152,256]{1,0:T(8,128)(2,1)S(1)}, bf16[1152,256]{1,0:T(8,128)(2,1)}, u32[]{:S(2)}, u32[]{:S(2)}) collective-permute-start(bf16[1152,256]{1,0:T(8,128)(2,1)S(1)} %collective-permute-done.6.refs_8_.refs_12_), channel_id=1, source_target_pairs={{0,16},{16,32},{32,48},{48,0},{1,17},{17,33},{33,49},{49,1},{2,18}... | collective-permute-start | bytes 1769480 | tf_op jit(solution)/shard_map/ppermute | solution.py:240
  47.6 18.9 %collective-permute-start.12 = (bf16[1152,256]{1,0:T(8,128)(2,1)S(1)}, bf16[1152,256]{1,0:T(8,128)(2,1)S(1)}, u32[]{:S(2)}, u32[]{:S(2)}) collective-permute-start(bf16[1152,256]{1,0:T(8,128)(2,1)S(1)} %collective-permute-done.6.refs_8_.refs_12_), channel_id=1, source_target_pairs={{0,64},{64,128},{128,192},{192,0},{1,65},{65,129},{129,193},{193,1... | collective-permute-start | bytes 1769480 | tf_op jit(solution)/shard_map/ppermute | solution.py:243
  48.5 18.9 %collective-permute-start.13 = (bf16[1152,256]{1,0:T(8,128)(2,1)S(1)}, bf16[1152,256]{1,0:T(8,128)(2,1)S(1)}, u32[]{:S(2)}, u32[]{:S(2)}) collective-permute-start(bf16[1152,256]{1,0:T(8,128)(2,1)S(1)} %collective-permute-done.6.refs_8_.refs_12_), channel_id=1, source_target_pairs={{0,192},{64,0},{128,64},{192,128},{1,193},{65,1},{129,65},{193,129... | collective-permute-start | bytes 1769480 | tf_op jit(solution)/shard_map/ppermute | solution.py:246
  57.7 1.0 copy-start.10
  64.9 1.6 %copy-start = (f32[2,2,640,256]{3,2,1,0:T(8,128)}, f32[2,2,640,256]{3,2,1,0:T(8,128)S(1)}, u32[]{:S(2)}) copy-start(f32[2,2,640,256]{3,2,1,0:T(8,128)S(1)} %shard_map.48.refs_12_) | copy-start | bytes 7864324
  66.5 0.8 copy-start.3
  67.3 0.8 copy-start.6
  68.2 20.1 %collective-permute-start.14 = (bf16[1152,256]{1,0:T(8,128)(2,1)S(1)}, bf16[1152,256]{1,0:T(8,128)(2,1)S(1)}, u32[]{:S(2)}, u32[]{:S(2)}) collective-permute-start(bf16[1152,256]{1,0:T(8,128)(2,1)S(1)} %constant_dynamic-update-slice_fusion.refs_11_.refs_15_), channel_id=1, source_target_pairs={{0,16},{16,32},{32,48},{48,0},{1,17},{17,33},{33,49},{49,1},{2,18}... | collective-permute-start | bytes 1769480 | tf_op jit(solution)/shard_map/ppermute | solution.py:240
  68.7 19.6 %collective-permute-start.15 = (bf16[1152,256]{1,0:T(8,128)(2,1)}, bf16[1152,256]{1,0:T(8,128)(2,1)S(1)}, u32[]{:S(2)}, u32[]{:S(2)}) collective-permute-start(bf16[1152,256]{1,0:T(8,128)(2,1)} %collective-permute-done.11.refs_6_.refs_9_), channel_id=1, source_target_pairs={{0,64},{64,128},{128,192},{192,0},{1,65},{65,129},{129,193},{193,1... | collective-permute-start | bytes 1769480 | tf_op jit(solution)/shard_map/ppermute | solution.py:243
  68.7 19.6 %collective-permute-start.16 = (bf16[1152,256]{1,0:T(8,128)(2,1)}, bf16[1152,256]{1,0:T(8,128)(2,1)S(1)}, u32[]{:S(2)}, u32[]{:S(2)}) collective-permute-start(bf16[1152,256]{1,0:T(8,128)(2,1)} %collective-permute-done.11.refs_6_.refs_9_), channel_id=1, source_target_pairs={{0,192},{64,0},{128,64},{192,128},{1,193},{65,1},{129,65},{193,129... | collective-permute-start | bytes 1769480 | tf_op jit(solution)/shard_map/ppermute | solution.py:246
  72.1 1.1 copy-start.4
  73.1 1.1 copy-start.7
  74.2 1.3 copy-start.11
  75.5 5.5 %copy-start.5 = (bf16[1152,256]{1,0:T(8,128)(2,1)S(1)}, bf16[1152,256]{1,0:T(8,128)(2,1)}, u32[]{:S(2)}) copy-start(bf16[1152,256]{1,0:T(8,128)(2,1)} %copy-done.3) | copy-start | bytes 1769476
  75.5 5.5 %copy-start.8 = (bf16[1152,256]{1,0:T(8,128)(2,1)S(1)}, bf16[1152,256]{1,0:T(8,128)(2,1)}, u32[]{:S(2)}) copy-start(bf16[1152,256]{1,0:T(8,128)(2,1)} %copy-done.6) | copy-start | bytes 1769476
  80.0 1.0 copy-start.12
  86.7 1.6 %copy-start.1 = (f32[2,2,640,256]{3,2,1,0:T(8,128)}, f32[2,2,640,256]{3,2,1,0:T(8,128)S(1)}, u32[]{:S(2)}) copy-start(f32[2,2,640,256]{3,2,1,0:T(8,128)S(1)} %shard_map.50.refs_12_) | copy-start | bytes 7864324
  88.3 18.4 %collective-permute-start.17 = (bf16[1152,256]{1,0:T(8,128)(2,1)S(1)}, bf16[1152,256]{1,0:T(8,128)(2,1)S(1)}, u32[]{:S(2)}, u32[]{:S(2)}) collective-permute-start(bf16[1152,256]{1,0:T(8,128)(2,1)S(1)} %collective-permute-done.14.refs_6_.refs_9_), channel_id=1, source_target_pairs={{0,16},{16,32},{32,48},{48,0},{1,17},{17,33},{33,49},{49,1},{2,18}... | collective-permute-start | bytes 1769480 | tf_op jit(solution)/shard_map/ppermute | solution.py:240
  89.7 17.1 %collective-permute-start.18 = (bf16[576,256]{1,0:T(8,128)(2,1)S(1)}, bf16[576,256]{1,0:T(8,128)(2,1)S(1)}, u32[]{:S(2)}, u32[]{:S(2)}) collective-permute-start(bf16[576,256]{1,0:T(8,128)(2,1)S(1)} %slice.43), channel_id=1, source_target_pairs={{0,64},{64,128},{128,192},{192,0},{1,65},{65,129},{129,193},{193,1... | collective-permute-start | bytes 884744 | tf_op jit(solution)/shard_map/ppermute | solution.py:243
  89.8 16.9 %collective-permute-start.19 = (bf16[576,256]{1,0:T(8,128)(2,1)S(1)}, bf16[576,256]{1,0:T(8,128)(2,1)S(1)}, u32[]{:S(2)}, u32[]{:S(2)}) collective-permute-start(bf16[576,256]{1,0:T(8,128)(2,1)S(1)} %slice.44), channel_id=1, source_target_pairs={{0,192},{64,0},{128,64},{192,128},{1,193},{65,1},{129,65},{193,129... | collective-permute-start | bytes 884744 | tf_op jit(solution)/shard_map/ppermute | solution.py:246
  95.4 1.3 copy-start.13
  106.8 4.3 %copy-start.9 = (f32[2,2,640,1]{3,2,1,0:T(8,128)S(1)}, f32[2,2,640,1]{3,2,1,0:T(8,128)}, u32[]{:S(2)}) copy-start(f32[2,2,640,1]{3,2,1,0:T(8,128)} %copy.5.column_ref) | copy-start | bytes 30724
  111.1 6.5 %copy-start.15 = (f32[2,2,640]{2,1,0:T(2,128)S(1)}, f32[2,2,640]{2,1,0:T(2,128)}, u32[]{:S(2)}) copy-start(f32[2,2,640]{2,1,0:T(2,128)} %copy-done.14) | copy-start | bytes 30724
  112.0 9.5 %collective-permute-start.20 = (bf16[2,144,128]{2,1,0:T(8,128)(2,1)S(1)}, bf16[2,144,128]{2,1,0:T(8,128)(2,1)S(1)}, u32[]{:S(2)}, u32[]{:S(2)}) collective-permute-start(bf16[2,144,128]{2,1,0:T(8,128)(2,1)S(1)} %get-tuple-element.82), channel_id=1, source_target_pairs={{0,16},{16,32},{32,48},{48,0},{1,17},{17,33},{33,49},{49,1},{2,18}... | collective-permute-start | bytes 221192 | tf_op jit(solution)/shard_map/ppermute | solution.py:279
  113.3 8.2 %collective-permute-start.21 = (bf16[2,144,128]{2,1,0:T(8,128)(2,1)S(1)}, bf16[2,144,128]{2,1,0:T(8,128)(2,1)S(1)}, u32[]{:S(2)}, u32[]{:S(2)}) collective-permute-start(bf16[2,144,128]{2,1,0:T(8,128)(2,1)S(1)} %get-tuple-element.82), channel_id=1, source_target_pairs={{0,32},{16,48},{32,0},{48,16},{1,33},{17,49},{33,1},{49,17},{2,34}... | collective-permute-start | bytes 221192 | tf_op jit(solution)/shard_map/ppermute | solution.py:279
  115.2 6.3 %collective-permute-start.22 = (bf16[2,144,128]{2,1,0:T(8,128)(2,1)S(1)}, bf16[2,144,128]{2,1,0:T(8,128)(2,1)S(1)}, u32[]{:S(2)}, u32[]{:S(2)}) collective-permute-start(bf16[2,144,128]{2,1,0:T(8,128)(2,1)S(1)} %get-tuple-element.82), channel_id=1, source_target_pairs={{0,48},{16,0},{32,16},{48,32},{1,49},{17,1},{33,17},{49,33},{2,50}... | collective-permute-start | bytes 221192 | tf_op jit(solution)/shard_map/ppermute | solution.py:279
  121.7 10.4 %collective-permute-start.23 = (bf16[2,144,128]{2,1,0:T(8,128)(2,1)S(1)}, bf16[2,144,128]{2,1,0:T(8,128)(2,1)S(1)}, u32[]{:S(2)}, u32[]{:S(2)}) collective-permute-start(bf16[2,144,128]{2,1,0:T(8,128)(2,1)S(1)} %get-tuple-element.87), channel_id=1, source_target_pairs={{0,64},{64,128},{128,192},{1,65},{65,129},{129,193},{2,66},{66,130... | collective-permute-start | bytes 221192 | tf_op jit(solution)/shard_map/ppermute | solution.py:283
  123.0 9.1 %collective-permute-start.24 = (bf16[2,144,128]{2,1,0:T(8,128)(2,1)S(1)}, bf16[2,144,128]{2,1,0:T(8,128)(2,1)S(1)}, u32[]{:S(2)}, u32[]{:S(2)}) collective-permute-start(bf16[2,144,128]{2,1,0:T(8,128)(2,1)S(1)} %get-tuple-element.87), channel_id=1, source_target_pairs={{0,128},{64,192},{1,129},{65,193},{2,130},{66,194},{3,131},{67,195... | collective-permute-start | bytes 221192 | tf_op jit(solution)/shard_map/ppermute | solution.py:283
  127.0 5.1 %collective-permute-start.25 = (bf16[2,144,128]{2,1,0:T(8,128)(2,1)S(1)}, bf16[2,144,128]{2,1,0:T(8,128)(2,1)S(1)}, u32[]{:S(2)}, u32[]{:S(2)}) collective-permute-start(bf16[2,144,128]{2,1,0:T(8,128)(2,1)S(1)} %get-tuple-element.87), channel_id=1, source_target_pairs={{0,192},{1,193},{2,194},{3,195},{4,196},{5,197},{6,198},{7,199},{8... | collective-permute-start | bytes 221192 | tf_op jit(solution)/shard_map/ppermute | solution.py:283
  134.3 17.5 %copy-start.17 = (f32[512]{0:T(512)S(1)}, f32[512]{0:T(512)}, u32[]{:S(2)}) copy-start(f32[512]{0:T(512)} %param.7) | copy-start | bytes 6148
  134.4 17.4 %collective-permute-start.26 = (f32[640,256]{1,0:T(8,128)S(1)}, f32[640,256]{1,0:T(8,128)S(1)}, u32[]{:S(2)}, u32[]{:S(2)}) collective-permute-start(f32[640,256]{1,0:T(8,128)S(1)} %get-tuple-element.100), channel_id=1, source_target_pairs={{0,8},{8,0},{1,9},{9,1},{2,10},{10,2},{3,11},{11,3},{4,12},{12,4},... | collective-permute-start | bytes 1966088 | tf_op jit(solution)/shard_map/ppermute | solution.py:291
  134.5 2.1 %collective-permute-start.27 = (f32[640]{0:T(1024)S(1)}, f32[640]{0:T(1024)S(1)}, u32[]{:S(2)}, u32[]{:S(2)}) collective-permute-start(f32[640]{0:T(1024)S(1)} %get-tuple-element.97), channel_id=1, source_target_pairs={{0,8},{8,0},{1,9},{9,1},{2,10},{10,2},{3,11},{11,3},{4,12},{12,4},... | collective-permute-start | bytes 7688 | tf_op jit(solution)/shard_map/ppermute | solution.py:290
  136.6 3.6 %collective-permute-start.28 = (f32[640]{0:T(1024)S(1)}, f32[640]{0:T(1024)S(1)}, u32[]{:S(2)}, u32[]{:S(2)}) collective-permute-start(f32[640]{0:T(1024)S(1)} %add.182), channel_id=1, source_target_pairs={{0,2},{2,4},{4,6},{6,0},{1,3},{3,5},{5,7},{7,1},{8,10},{10,12},{12... | collective-permute-start | bytes 7688 | tf_op jit(solution)/shard_map/ppermute | solution.py:292
  136.8 5.1 %collective-permute-start.29 = (f32[640]{0:T(1024)S(1)}, f32[640]{0:T(1024)S(1)}, u32[]{:S(2)}, u32[]{:S(2)}) collective-permute-start(f32[640]{0:T(1024)S(1)} %add.182), channel_id=1, source_target_pairs={{0,4},{2,6},{4,0},{6,2},{1,5},{3,7},{5,1},{7,3},{8,12},{10,14},{12... | collective-permute-start | bytes 7688 | tf_op jit(solution)/shard_map/ppermute | solution.py:292
  139.4 4.8 %collective-permute-start.30 = (f32[640]{0:T(1024)S(1)}, f32[640]{0:T(1024)S(1)}, u32[]{:S(2)}, u32[]{:S(2)}) collective-permute-start(f32[640]{0:T(1024)S(1)} %add.182), channel_id=1, source_target_pairs={{0,6},{2,0},{4,2},{6,4},{1,7},{3,1},{5,3},{7,5},{8,14},{10,8},{12,... | collective-permute-start | bytes 7688 | tf_op jit(solution)/shard_map/ppermute | solution.py:292
  144.2 7.5 %collective-permute-start.31 = (f32[640]{0:T(1024)S(1)}, f32[640]{0:T(1024)S(1)}, u32[]{:S(2)}, u32[]{:S(2)}) collective-permute-start(f32[640]{0:T(1024)S(1)} %add_add_fusion), channel_id=1, source_target_pairs={{0,1},{1,0},{2,3},{3,2},{4,5},{5,4},{6,7},{7,6},{8,9},{9,8},{10,11... | collective-permute-start | bytes 7688 | tf_op jit(solution)/shard_map/ppermute | solution.py:293
